TPU v7x, 512 devices: a whole 4x8x8 slice. The times are simulated.
512 devices in a mesh: gx: 16 (over z, x_lo), vert: 32 (over y, x_hi, core).
Axes of the slice: x: 4 (x_hi: 2, x_lo: 2; x = x_hi * 2 + x_lo), y: 8, z: 8, core: 2. Of those that a mesh axis runs over, the one named last changes fastest.
Arguments:
- dist: bfloat16 [1024, 32, 4096], P('vert', 'gx'), may hold values from 0.02 to 6
- vel_index: int32 [3, 1024], P(None, 'vert'), may hold values from 0 to 32, as said below
- weight_int: int32 [1024], P('vert'), may hold values from 1024 to 65535
Outputs:
- advanced: bfloat16 [1024, 32, 4096], P('vert', 'gx')
Inputs may be any that keep to these rules, and one draw needn't show every extreme that they name: `vel_index`: in each of the three rows every node index occurs 1024 // 33 or 1024 // 33 + 1 times.
All inputs are finite; a program needn't handle non-finite values.
Results may differ from a plain program's by a relative error of at most 0.0038.
Values may be sent and summed in bfloat16 or wider, within the bound.
No kernel may reach another device: no remote copies, remote signals or barrier semaphores. Data moves between devices by JAX's collectives and lax.ppermute only.
A program may use at most 64 MiB of HBM per device.

v0:
```python
import jax
import jax.numpy as jnp
from jax import lax
from jax.sharding import PartitionSpec as P

NV = 1024
NODES = 33
NY = 64
NZ = 64


speed_max = 4.0
time_step = 1.0 / 12.0
relax_coef = 0.1


def padded_2(block, sides, width):
    for axis, dim in sides:
        count = lax.axis_size(axis)
        forward = [(i, i + 1) for i in range(count - 1)]
        forward.append((count - 1, 0))
        backward = [(target, source) for source, target in forward]
        low = lax.ppermute(
            lax.slice_in_dim(block, block.shape[dim] - width, None, axis=dim), axis, forward
        )
        high = lax.ppermute(lax.slice_in_dim(block, 0, width, axis=dim), axis, backward)
        block = jnp.concatenate([low, block, high], axis=dim)
    return block


def velocities(vel_index):
    nodes = speed_max * jnp.cos(jnp.pi * jnp.arange(NODES, dtype=jnp.float32) / (NODES - 1))
    onehot = (vel_index[:, :, None] == jnp.arange(NODES, dtype=jnp.int32)[None, None, :]).astype(
        jnp.float32
    )
    return jnp.sum(onehot * nodes[None, None, :], axis=2)


def moment_rows(speeds, weight_int):
    weight = weight_int.astype(jnp.float32) * (512.0 / (32768.0 * NV))
    square = speeds[0] * speeds[0] + speeds[1] * speeds[1] + speeds[2] * speeds[2]
    return jnp.stack(
        [weight, weight * speeds[0], weight * speeds[1], weight * speeds[2], weight * square]
    )


def maxwell_params(moments):
    density = moments[0]
    flow = moments[1:4] / density[None]
    temper = (moments[4] / density - jnp.sum(flow * flow, axis=0)) / 3.0
    scale = density * jnp.power(2.0 * jnp.pi * temper, -1.5)
    rate = time_step * relax_coef * density * jnp.sqrt(temper)
    return jnp.concatenate([flow, temper[None], scale[None], rate[None]], axis=0)


def collide(dist, speeds, params):
    grid = params.reshape(6, dist.shape[1], dist.shape[2])
    spread = jnp.zeros(dist.shape, jnp.float32)
    for comp in range(3):
        diff = speeds[comp][:, None, None] - grid[comp][None]
        spread = spread + diff * diff
    equil = grid[4][None] * jnp.exp(-spread / (2.0 * grid[3][None]))
    rate = grid[5][None]
    return ((dist.astype(jnp.float32) + rate * equil) / (1.0 + rate)).astype(jnp.bfloat16)


def stream(padded, speeds):
    values = padded.astype(jnp.float32)
    center = values[:, 1:-1]
    lower = values[:, :-2]
    upper = values[:, 2:]
    speed_x = speeds[0][:, None, None]
    flux = jnp.maximum(speed_x, 0.0) * (center - lower) + jnp.minimum(speed_x, 0.0) * (
        upper - center
    )
    count_v = center.shape[0]
    planes = center.shape[1]
    cube = center.reshape(count_v, planes, NY, NZ)
    for comp, dim in ((1, 2), (2, 3)):
        speed_k = speeds[comp][:, None, None, None]
        part = jnp.maximum(speed_k, 0.0) * (cube - jnp.roll(cube, 1, dim)) + jnp.minimum(
            speed_k, 0.0
        ) * (jnp.roll(cube, -1, dim) - cube)
        flux = flux + part.reshape(count_v, planes, NY * NZ)
    return (center - time_step * flux).astype(jnp.bfloat16)


def shards(dist, vel_index, weight_int):
    speeds = velocities(vel_index)
    rows = moment_rows(speeds, weight_int)
    count_v = dist.shape[0]
    partial_value = jnp.dot(
        rows, dist.reshape(count_v, -1).astype(jnp.float32), precision=lax.Precision.HIGHEST
    )
    summed = lax.psum(partial_value, "vert")
    params = maxwell_params(summed)
    relaxed = collide(dist, speeds, params)
    padded = padded_2(relaxed, (("gx", 1),), 1)
    return stream(padded, speeds)


def solution(mesh):
    return jax.shard_map(
        shards,
        mesh=mesh,
        in_specs=(P("vert", "gx", None), P(None, "vert"), P("vert")),
        out_specs=P("vert", "gx", None),
        check_vma=False,
    )
```

profile of v0, /device:TPU:1, one launch (start us, length us, event | category | flops | bytes accessed | tf_op | source)
XLA Modules:
  0.0 368.8 jit_solution(10877122980106615199)
XLA Ops:
  6.5 0.0 copy-start.2
  6.5 0.0 all-reduce.2.cloned.1.call-start
  6.6 1.4 copy.4
  8.0 0.8 select_reduce_fusion
  8.8 0.7 broadcast_maximum_fusion.2
  9.5 1.0 fusion.13
  10.5 0.0 all-reduce.2.cloned.1.call-update
  10.6 276.9 %all-reduce.2.cloned.1.call-done = f32[5,8192]{1,0:T(8,128)} async-done(((f32[5,8192]{1,0:T(8,128)}), f32[5,8192]{1,0:T(8,128)}) %all-reduce.2.cloned.1.call-update) | async-done | bytes 163856 | tf_op jit(solution)/shard_map/psum | solution.py:95
  287.5 1.1 fusion.12
  288.6 1.1 multiply_reduce_fusion
  289.7 0.5 broadcast.121
  290.2 2.3 slice_reduce_fusion.2
  292.6 0.1 broadcast_add_fusion
  292.7 0.0 copy-done.2
  292.7 2.7 fusion.5
  295.4 1.2 fusion.11
  296.6 2.2 collective-permute-start
  298.8 5.5 %collective-permute-start.1 = (bf16[32,1,4096]{2,1,0:T(2,128)(2,1)S(1)}, bf16[32,1,4096]{2,1,0:T(2,128)(2,1)S(1)}, u32[]{:S(2)}, u32[]{:S(2)}) collective-permute-start(bf16[32,1,4096]{2,1,0:T(2,128)(2,1)S(1)} %get-tuple-element.25), channel_id=1, source_target_pairs={{32,0},{64,32},{96,64},{128,96},{160,128},{192,160},{224,192},{256... | collective-permute-start | bytes 786440 | tf_op jit(solution)/shard_map/ppermute | solution.py:26
  304.3 15.8 %collective-permute-done = bf16[32,1,4096]{2,1,0:T(2,128)(2,1)S(1)} collective-permute-done((bf16[32,1,4096]{2,1,0:T(2,128)(2,1)S(1)}, bf16[32,1,4096]{2,1,0:T(2,128)(2,1)S(1)}, u32[]{:S(2)}, u32[]{:S(2)}) %collective-permute-start) | collective-permute-done | bytes 262176 | tf_op jit(solution)/shard_map/ppermute | solution.py:23
  320.1 5.7 %collective-permute-done.1 = bf16[32,1,4096]{2,1,0:T(2,128)(2,1)S(1)} collective-permute-done((bf16[32,1,4096]{2,1,0:T(2,128)(2,1)S(1)}, bf16[32,1,4096]{2,1,0:T(2,128)(2,1)S(1)}, u32[]{:S(2)}, u32[]{:S(2)}) %collective-permute-start.1) | collective-permute-done | bytes 262176 | tf_op jit(solution)/shard_map/ppermute | solution.py:26
  325.8 1.6 maximum_convert_fusion
  327.4 0.0 copy-start
  327.4 1.3 copy-done
  328.8 0.6 slice.128
  329.4 1.2 reshape.130
  330.5 1.9 fusion.8
  332.4 2.7 fusion.9
  335.1 2.9 fusion.10
  338.0 0.5 pad_maximum_fusion
  338.5 1.1 concatenate.30
  339.6 1.8 pad_maximum_fusion.1
  341.4 2.0 concatenate.32
  343.4 2.8 pad_maximum_fusion.2
  346.2 2.1 concatenate.34
  348.3 4.2 %pad_maximum_fusion.3 = f32[32,2,64,64]{3,2,1,0:T(8,128)} fusion(f32[32,2,64,1]{3,2,1,0:T(8,128)} %get-tuple-element.21, f32[32,2,64,63]{3,2,1,0:T(8,128)} %get-tuple-element.23), kind=kLoop, calls=%fused_computation.3 | loop fusion | flops 262144 | bytes 2097152 | tf_op jit(solution)/shard_map/jit(_roll_static)/concatenate | solution.py:83
  352.5 0.0 copy-start.1
  352.5 3.3 concatenate.36
  355.9 0.0 copy-done.1
  355.9 6.1 %subtract_convert_fusion = bf16[32,2,4096]{2,1,0:T(2,128)(2,1)} fusion(f32[32,4,4096]{2,1,0:T(4,128)S(1)} %copy-done.1, f32[32,2,4096]{2,1,0:T(2,128)} %concatenate.36, f32[32,2,4096]{2,1,0:T(2,128)} %concatenate.34, f32[32,2,4096]{2,1,0:T(2,128)} %concatenate.32, f32[32,2,4096]{2,1,0:T(2,128)S(1)} %concatenate.30, f32[32]{0:T(128)S(1)} %get-tuple-element.34, ...), kind=kLoop, calls=%fused_computation.12 | loop fusion | flops 5242880 | bytes 7865088 | tf_op jit(solution)/shard_map/convert_element_type | solution.py:85
  (12 shorter events, 0.3 us)
Async XLA Ops:
  6.5 286.2 %copy-start.2 = (bf16[32,2,4096]{2,1,0:T(2,128)(2,1)S(1)}, bf16[32,2,4096]{2,1,0:T(2,128)(2,1)}, u32[]{:S(2)}) copy-start(bf16[32,2,4096]{2,1,0:T(2,128)(2,1)} %param.3) | copy-start | bytes 1572868
  6.5 280.9 %all-reduce.2.cloned.1.call-start = ((), (), s32[]{:S(2)}) async-start(), calls=%async_computation | async-start | bytes 524288 | tf_op jit(solution)/shard_map/psum | solution.py:95
  296.6 23.5 %collective-permute-start = (bf16[32,1,4096]{2,1,0:T(2,128)(2,1)S(1)}, bf16[32,1,4096]{2,1,0:T(2,128)(2,1)S(1)}, u32[]{:S(2)}, u32[]{:S(2)}) collective-permute-start(bf16[32,1,4096]{2,1,0:T(2,128)(2,1)S(1)} %get-tuple-element.24), channel_id=1, source_target_pairs={{0,32},{32,64},{64,96},{96,128},{128,160},{160,192},{192,224},{224... | collective-permute-start | bytes 786440 | tf_op jit(solution)/shard_map/ppermute | solution.py:23
  298.8 27.0 %collective-permute-start.1 = (bf16[32,1,4096]{2,1,0:T(2,128)(2,1)S(1)}, bf16[32,1,4096]{2,1,0:T(2,128)(2,1)S(1)}, u32[]{:S(2)}, u32[]{:S(2)}) collective-permute-start(bf16[32,1,4096]{2,1,0:T(2,128)(2,1)S(1)} %get-tuple-element.25), channel_id=1, source_target_pairs={{32,0},{64,32},{96,64},{128,96},{160,128},{192,160},{224,192},{256... | collective-permute-start | bytes 786440 | tf_op jit(solution)/shard_map/ppermute | solution.py:26
  327.4 1.4 copy-start
  352.5 3.3 copy-start.1
Sparse Core Ops, SparseCore 0:
  10.7 276.7 all-reduce.1
where the time goes:
time: 369 us
  waiting for transfers between devices  298 us (81%)
  other arithmetic  25.8 us (7%)
  local copies, waits for them, and re-layouts  22.4 us (6%)
  between operations  13.6 us (4%)
  starting transfers between devices  7.69 us (2%)
    psum x1, waiting for transfers between devices, shards(): summed = lax.psum(partial_value, 'vert')  277 us
    ppermute x1, waiting for transfers between devices, padded_2(): lax.ppermute(lax.slice_in_dim(block, block.shape[dim] - width, None, axis...  15.8 us
    slice x4, local copies, waits for them, and re-layouts, stream(): jnp.roll(cube, 1, dim)  7.48 us
  transfers between devices with their start and end apart: 3, of which 3 were waited for; matrix products, arithmetic and copies ran while one was open for 0% of the time, Pallas kernels for 0%

commit v1 on v0

v1 whole, which is shorter than its diff:
```python
import jax
import jax.numpy as jnp
import numpy as np
from jax import lax
from jax.experimental import pallas as pl
from jax.experimental.pallas import tpu as pltpu
from jax.sharding import Mesh, PartitionSpec as P

NV = 1024
NODES = 33
ROWS = 32
LANES = 128
CELLS = (ROWS, LANES)

speed_max = 4.0
time_step = 1.0 / 12.0
relax_coef = 0.1
center = 24.0
log2e = 1.4426950408889634

SIZES = (8, 2, 8, 2, 2)
NAMES = ("z", "xl", "y", "xh", "core")
GX = ("z", "xl")
VERT = ("y", "xh", "core")
QUAD = ("z", "xl", "xh", "core")

VMEM = pl.BlockSpec(memory_space=pltpu.VMEM)
SMEM = pl.BlockSpec(memory_space=pltpu.SMEM)


def quad_place(z, xl, xh, core):
    return ((z % SIZES[0]) * 2 + xl) * 4 + xh * 2 + core


QUADS = [
    [quad_place(z, xl, xh, 0) for xl in range(2) for xh in range(2)] for z in range(SIZES[0])
] + [
    [quad_place(z + 1 - xl, xl, xh, 1) for xl in (1, 0) for xh in range(2)]
    for z in range(SIZES[0])
]


def node_table():
    steps = np.arange(NODES, dtype=np.float64) / (NODES - 1)
    return jnp.asarray(speed_max * np.cos(np.pi * steps), jnp.float32)


def moments_kernel(index_ref, weight_ref, node_ref, low_ref, high_ref, out_ref):
    for plane, ref in enumerate((low_ref, high_ref)):
        sums = [jnp.zeros(CELLS, jnp.float32) for _ in range(5)]
        for v in range(ref.shape[0]):
            sx = node_ref[index_ref[0, v]]
            sy = node_ref[index_ref[1, v]]
            sz = node_ref[index_ref[2, v]]
            weight = weight_ref[v].astype(jnp.float32) * (512.0 / (32768.0 * NV))
            square = sx * sx + sy * sy + sz * sz
            factors = (weight, weight * sx, weight * sy, weight * sz, weight * (square - center))
            value = ref[v].astype(jnp.float32)
            sums = [total + factor * value for total, factor in zip(sums, factors)]
        for comp in range(5):
            out_ref[plane, comp] = sums[comp]


def chip_kernel(plane_ref, both_ref, out_ref):
    plane = plane_ref[0]
    for comp in range(5):
        total = (both_ref[0, plane, comp] + both_ref[1, plane, comp]).astype(out_ref.dtype)
        for copy in range(out_ref.shape[0]):
            out_ref[copy, comp] = total


def column_kernel(parts_ref, out_ref):
    for comp in range(5):
        total = parts_ref[0, comp].astype(jnp.float32)
        for part in range(1, parts_ref.shape[0]):
            total = total + parts_ref[part, comp].astype(jnp.float32)
        for copy in range(out_ref.shape[0]):
            out_ref[copy, comp] = total


def advance_kernel(
    side_ref, index_ref, node_ref, sums_ref, before_ref, low_ref, high_ref, after_ref,
    out_low_ref, out_high_ref, params_ref,
):
    side = side_ref[0]
    for plane in range(4):
        half, pair = plane // 2, 2 * (plane % 2)
        half = half + (1 - side) * (1 - 2 * half)
        total = [sums_ref[half, pair, comp] + sums_ref[half, pair + 1, comp] for comp in range(5)]
        density = total[0]
        inverse = 1.0 / density
        flow = [total[comp] * inverse for comp in (1, 2, 3)]
        speed2 = flow[0] * flow[0] + flow[1] * flow[1] + flow[2] * flow[2]
        temper = (total[4] * inverse + center - speed2) * (1.0 / 3.0)
        root = jnp.sqrt(temper)
        rate = (time_step * relax_coef) * density * root
        scale = density * ((2.0 * np.pi) ** -1.5) / (temper * root)
        keep = 1.0 / (1.0 + rate)
        for comp in range(3):
            params_ref[plane, comp] = flow[comp]
        params_ref[plane, 3] = (-0.5 * log2e) / temper
        params_ref[plane, 4] = scale * (rate * keep)
        params_ref[plane, 5] = keep

    lane = lax.broadcasted_iota(jnp.int32, CELLS, 1)

    def relax(value, plane, sx, sy, sz):
        dx = sx - params_ref[plane, 0]
        dy = sy - params_ref[plane, 1]
        dz = sz - params_ref[plane, 2]
        spread = dx * dx + dy * dy + dz * dz
        equil = params_ref[plane, 4] * jnp.exp2(spread * params_ref[plane, 3])
        mixed = value.astype(jnp.float32) * params_ref[plane, 5] + equil
        return mixed.astype(jnp.bfloat16).astype(jnp.float32)

    def step(v, carry):
        sx = node_ref[index_ref[0, v]]
        sy = node_ref[index_ref[1, v]]
        sz = node_ref[index_ref[2, v]]
        up_x, up_y, up_z = sx > 0.0, sy > 0.0, sz > 0.0
        ax, ay, az = (time_step * jnp.abs(s) for s in (sx, sy, sz))
        rest = 1.0 - (ax + ay + az)
        edge_value = jnp.where(up_x, before_ref[v].astype(jnp.float32), after_ref[v].astype(jnp.float32))
        edge = relax(edge_value, jnp.where(up_x, 0, 3), sx, sy, sz)
        low = relax(low_ref[v], 1, sx, sy, sz)
        high = relax(high_ref[v], 2, sx, sy, sz)
        from_x = (jnp.where(up_x, edge, high), jnp.where(up_x, low, edge))
        shift_z = jnp.where(up_z, 1, LANES - 1)
        wrap_z = (lane & 63) == jnp.where(up_z, 0, 63)
        wrap_y = (lane >> 6) == jnp.where(up_y, 0, 1)
        for value, beside, ref in ((low, from_x[0], out_low_ref), (high, from_x[1], out_high_ref)):
            swapped = pltpu.roll(value, 64, 1)
            row = jnp.where(up_y, pltpu.roll(swapped, 1, 0), pltpu.roll(swapped, ROWS - 1, 0))
            from_y = jnp.where(wrap_y, row, swapped)
            near = pltpu.roll(value, shift_z, 1)
            from_z = jnp.where(wrap_z, pltpu.roll(near, 64, 1), near)
            moved = rest * value + ax * beside + ay * from_y + az * from_z
            ref[v] = moved.astype(jnp.bfloat16)
        return carry

    lax.fori_loop(0, low_ref.shape[0], step, 0, unroll=2)


def shards(dist, vel_index, weight_int):
    count_v = dist.shape[0]
    nodes = node_table()
    side = lax.axis_index("xl")
    core = lax.axis_index("core")
    plane = jnp.reshape(1 ^ side ^ core, (1,)).astype(jnp.int32)
    side = jnp.reshape(side, (1,)).astype(jnp.int32)
    f32, bf16 = jnp.float32, jnp.bfloat16

    planes = dist.reshape(count_v, 2, ROWS, LANES)
    low, high = planes[:, 0], planes[:, 1]
    count = SIZES[0] * SIZES[1]
    forward = [(i, (i + 1) % count) for i in range(count)]
    backward = [(target, source) for source, target in forward]
    before = lax.ppermute(high, GX, forward)
    after = lax.ppermute(low, GX, backward)

    partial_sums = pl.pallas_call(
        moments_kernel,
        out_shape=jax.ShapeDtypeStruct((2, 5) + CELLS, f32),
        in_specs=[SMEM, SMEM, SMEM, VMEM, VMEM],
        out_specs=VMEM,
        name="moments",
    )(vel_index, weight_int, nodes, low, high)
    both = lax.all_gather(partial_sums, "core")
    chip = pl.pallas_call(
        chip_kernel,
        out_shape=jax.ShapeDtypeStruct((SIZES[2], 5) + CELLS, bf16),
        in_specs=[SMEM, VMEM],
        out_specs=VMEM,
        name="chip_sum",
    )(plane, both)
    parts = lax.all_to_all(chip, "y", 0, 0)
    column = pl.pallas_call(
        column_kernel,
        out_shape=jax.ShapeDtypeStruct((4, 5) + CELLS, f32),
        in_specs=[VMEM],
        out_specs=VMEM,
        name="column_sum",
    )(parts)
    quad = lax.all_to_all(column, QUAD, 0, 0, axis_index_groups=QUADS)
    sums = lax.all_gather(quad, "core")
    shape = jax.ShapeDtypeStruct((count_v,) + CELLS, bf16)
    out_low, out_high = pl.pallas_call(
        advance_kernel,
        out_shape=(shape, shape),
        in_specs=[SMEM, SMEM, SMEM, VMEM, VMEM, VMEM, VMEM, VMEM],
        out_specs=(VMEM, VMEM),
        scratch_shapes=[pltpu.VMEM((4, 6) + CELLS, f32)],
        name="advance",
    )(side, vel_index, nodes, sums, before, low, high, after)
    return jnp.stack([out_low, out_high], axis=1).reshape(dist.shape)


def solution(mesh):
    parts = Mesh(mesh.devices.reshape(SIZES), NAMES)
    return jax.shard_map(
        shards,
        mesh=parts,
        in_specs=(P(VERT, GX, None), P(None, VERT), P(VERT)),
        out_specs=P(VERT, GX, None),
        check_vma=False,
    )
```

time: 369 us -> 72 us (0.20)
  waiting for transfers between devices: 298 us -> 4.36 us
  blocking collectives: 0 us -> 31.2 us
  other arithmetic: 25.8 us -> 1.99 us
  local copies, waits for them, and re-layouts: 22.4 us -> 5.12 us
  between operations: 13.6 us -> 0.06 us
  Pallas kernels: 0 us -> 11.1 us
  starting transfers between devices: 7.69 us -> 17.5 us
    psum x1 -> x0, waiting for transfers between devices: 277 us -> none  [shards(): summed = lax.psum(partial_value, 'vert')]
    ppermute x2, waiting for transfers between devices: 21.5 us -> 1.4 us  [the longest x1 1.4 us: shards(): after = lax.ppermute(low, GX, backward)]
    all_to_all x0 -> x1, blocking collectives: none -> 17.8 us  [shards(): parts = lax.all_to_all(chip, 'y', 0, 0)]
    all_gather x0 -> x2, blocking collectives: none -> 13.4 us  [the longest x1 11 us: shards(): both = lax.all_gather(partial_sums, 'core')]
    pallas_call x0 -> x4, Pallas kernels: none -> 11.1 us  [the longest x1 5.31 us: shards(): pl.pallas_call(advance_kernel, out_shape=(shape, shape), in_specs=[SMEM,...]
    convert_element_type x3 -> x0, other arithmetic: 10.5 us -> none  [the longest x1 6.1 us: stream(): return (center - time_step * flux).astype(jnp.bfloat16)]
    all_to_all x0 -> x1, starting transfers between devices: none -> 10.1 us  [shards(): quad = lax.all_to_all(column, QUAD, 0, 0, axis_index_groups=QUADS)]
    concatenate x4 -> x0, other arithmetic: 9.29 us -> none  [the longest x2 5.97 us: stream(): jnp.roll(cube, -1, dim) - cube]
  transfers between devices with their start and end apart: 3 -> 3, of which waited for: 3 -> 2; matrix products, arithmetic and copies ran while one was open for 0% -> 0% of each run, Pallas kernels for 0% -> 0%
where the time goes in v1:
time: 72 us; the launch traced here: 71.3 us
  blocking collectives  31.2 us (43%)
  starting transfers between devices  17.5 us (24%)
  Pallas kernels  11.1 us (15%)
  local copies, waits for them, and re-layouts  5.12 us (7%)
  waiting for transfers between devices  4.36 us (6%)
  other arithmetic  1.99 us (3%)
    all_to_all x1, blocking collectives, shards(): parts = lax.all_to_all(chip, 'y', 0, 0)  17.8 us
    all_gather x1, blocking collectives, shards(): both = lax.all_gather(partial_sums, 'core')  11 us
    all_to_all x1, starting transfers between devices, shards(): quad = lax.all_to_all(column, QUAD, 0, 0, axis_index_groups=QUADS)  10.1 us
    ppermute x1, starting transfers between devices, shards(): after = lax.ppermute(low, GX, backward)  5.47 us
    pallas_call x1, Pallas kernels, shards(): pl.pallas_call(advance_kernel, out_shape=(shape, shape), in_specs=[SMEM,...  5.31 us
    all_to_all x1, waiting for transfers between devices, shards(): quad = lax.all_to_all(column, QUAD, 0, 0, axis_index_groups=QUADS)  2.96 us
    all_gather x1, blocking collectives, shards(): sums = lax.all_gather(quad, 'core')  2.4 us
    pallas_call x1, Pallas kernels, shards(): pl.pallas_call(moments_kernel, out_shape=jax.ShapeDtypeStruct((2, 5) + CE...  2.34 us
  transfers between devices with their start and end apart: 3, of which 2 were waited for; matrix products, arithmetic and copies ran while one was open for 0% of the time, Pallas kernels for 0%

profile of v1, /device:TPU:1, one launch (start us, length us, event | category | flops | bytes accessed | tf_op | source)
XLA Modules:
  0.0 71.3 jit_solution(8100838308288494594)
XLA Ops:
  0.0 1.4 %reshape.19 = bf16[32,2,32,128]{3,2,1,0:T(8,128)(2,1)S(1)} reshape(bf16[32,2,4096]{2,1,0:T(2,128)(2,1)} %param.4) | data formatting | bytes 1048576 | tf_op jit(solution)/shard_map/reshape | solution.py:153
  1.4 0.8 %slice_bitcast_fusion = (bf16[32,32,128]{2,1,0:T(8,128)(2,1)}, bf16[32,32,128]{2,1,0:T(8,128)(2,1)}) fusion(bf16[32,2,32,128]{3,2,1,0:T(8,128)(2,1)S(1)} %reshape.19), kind=kLoop, calls=%fused_computation.1 | loop fusion | bytes 1048576 | tf_op jit(solution)/shard_map/squeeze | solution.py:154
  2.3 2.3 %moments.1 = f32[2,5,32,128]{3,2,1,0:T(8,128)} custom-call(s32[3,32]{1,0:T(4,128)} %index_ref.3, s32[32]{0:T(128)} %weight_ref.1, f32[33]{0:T(128)} %constant.12.clone.node_ref, bf16[32,32,128]{2,1,0:T(8,128)(2,1)} %get-tuple-element.10.low_ref, bf16[32,32,128]{2,1,0:T(8,128)(2,1)} %get-tuple-element.9.high_ref), custom_call_target="tpu_custom_call" | custom-call | tf_op jit(solution)/shard_map/moments/pallas_call | solution.py:161
  4.6 11.0 %all-gather = f32[4,5,32,128]{3,2,1,0:T(8,128)} all-gather(f32[2,5,32,128]{3,2,1,0:T(8,128)} %moments.1), channel_id=2, replica_groups=mesh['z'=8,'xl'=2,'y'=8,'xh'=2,'core'=2] {'core'}, dimensions={0}, use_global_device_ids=true | all-gather | bytes 491520 | tf_op jit(solution)/shard_map/all_gather | solution.py:168
  15.6 1.7 %chip_sum.1 = bf16[8,5,32,128]{3,2,1,0:T(8,128)(2,1)} custom-call(s32[1]{0:T(128)} %bitcast.1.plane_ref, f32[2,2,5,32,128]{4,3,2,1,0:T(8,128)} %bitcast.13), custom_call_target="tpu_custom_call" | custom-call | tf_op jit(solution)/shard_map/chip_sum/pallas_call | solution.py:169
  17.3 17.8 %all_to_all.10.parts_ref = bf16[8,5,32,128]{3,2,1,0:T(8,128)(2,1)} all-to-all(bf16[8,5,32,128]{3,2,1,0:T(8,128)(2,1)} %chip_sum.1), channel_id=1, replica_groups=mesh['z'=8,'xl'=2,'y'=8,'xh'=2,'core'=2] {'y'}, dimensions={0} | all-to-all | bytes 655360 | tf_op jit(solution)/shard_map/all_to_all | solution.py:176
  35.2 1.7 %column_sum.1 = f32[4,5,32,128]{3,2,1,0:T(8,128)} custom-call(bf16[8,5,32,128]{3,2,1,0:T(8,128)(2,1)} %all_to_all.10.parts_ref), custom_call_target="tpu_custom_call" | custom-call | tf_op jit(solution)/shard_map/column_sum/pallas_call | solution.py:177
  36.9 0.0 copy-start
  36.9 0.0 copy-start.1
  36.9 10.1 %all-to-all-start.1 = ((f32[4,5,32,128]{3,2,1,0:T(8,128)}), f32[4,5,32,128]{3,2,1,0:T(8,128)S(1)}, u32[]{:S(2)}, u32[]{:S(2)}) async-start(f32[4,5,32,128]{3,2,1,0:T(8,128)} %column_sum.1), calls=%async_computation.1 | async-start | bytes 655360 | tf_op jit(solution)/shard_map/all_to_all | solution.py:184
  47.0 0.0 copy-done
  47.0 1.9 %collective-permute-start = (bf16[32,32,128]{2,1,0:T(8,128)(2,1)S(1)}, bf16[32,32,128]{2,1,0:T(8,128)(2,1)S(1)}, u32[]{:S(2)}, u32[]{:S(2)}) collective-permute-start(bf16[32,32,128]{2,1,0:T(8,128)(2,1)S(1)} %copy-done), channel_id=1, source_target_pairs={{0,32},{32,64},{64,96},{96,128},{128,160},{160,192},{192,224},{224... | collective-permute-start | bytes 786440 | tf_op jit(solution)/shard_map/ppermute | solution.py:158
  48.9 0.0 copy-done.1
  48.9 5.5 %collective-permute-start.1 = (bf16[32,32,128]{2,1,0:T(8,128)(2,1)S(1)}, bf16[32,32,128]{2,1,0:T(8,128)(2,1)S(1)}, u32[]{:S(2)}, u32[]{:S(2)}) collective-permute-start(bf16[32,32,128]{2,1,0:T(8,128)(2,1)S(1)} %copy-done.1), channel_id=1, source_target_pairs={{32,0},{64,32},{96,64},{128,96},{160,128},{192,160},{224,192},{256... | collective-permute-start | bytes 786440 | tf_op jit(solution)/shard_map/ppermute | solution.py:159
  54.4 3.0 %all-to-all-done.1 = f32[4,5,32,128]{3,2,1,0:T(8,128)S(1)} async-done(((f32[4,5,32,128]{3,2,1,0:T(8,128)}), f32[4,5,32,128]{3,2,1,0:T(8,128)S(1)}, u32[]{:S(2)}, u32[]{:S(2)}) %all-to-all-start.1) | async-done | bytes 327712 | tf_op jit(solution)/shard_map/all_to_all | solution.py:184
  57.3 2.4 %all-gather.1 = f32[8,5,32,128]{3,2,1,0:T(8,128)} all-gather(f32[4,5,32,128]{3,2,1,0:T(8,128)S(1)} %all-to-all-done.1), channel_id=3, replica_groups=mesh['z'=8,'xl'=2,'y'=8,'xh'=2,'core'=2] {'core'}, dimensions={0}, use_global_device_ids=true | all-gather | bytes 983040 | tf_op jit(solution)/shard_map/all_gather | solution.py:185
  59.7 0.0 collective-permute-done.before_ref
  59.7 0.0 copy-start.3
  59.7 1.4 %collective-permute-done.1.after_ref = bf16[32,32,128]{2,1,0:T(8,128)(2,1)S(1)} collective-permute-done((bf16[32,32,128]{2,1,0:T(8,128)(2,1)S(1)}, bf16[32,32,128]{2,1,0:T(8,128)(2,1)S(1)}, u32[]{:S(2)}, u32[]{:S(2)}) %collective-permute-start.1) | collective-permute-done | bytes 262176 | tf_op jit(solution)/shard_map/ppermute | solution.py:159
  61.1 0.0 copy-start.4
  61.1 0.0 copy-done.3
  61.2 0.7 copy-done.4
  61.9 5.3 %advance.1 = (bf16[32,32,128]{2,1,0:T(8,128)(2,1)}, bf16[32,32,128]{2,1,0:T(8,128)(2,1)}) custom-call(s32[1]{0:T(128)} %bitcast.side_ref, s32[3,32]{1,0:T(4,128)} %index_ref.3, f32[33]{0:T(128)} %constant.12.clone.node_ref, f32[2,4,5,32,128]{4,3,2,1,0:T(8,128)} %bitcast.12, bf16[32,32,128]{2,1,0:T(8,128)(2,1)} %copy-done.3, ...), custom_call_target="tpu_custom_call" | custom-call | tf_op jit(solution)/shard_map/advance/pallas_call | solution.py:187
  67.2 0.0 copy-start.2
  67.2 2.0 %stack.12 = bf16[32,1,4096]{2,1,0:T(2,128)(2,1)S(1)} reshape(bf16[32,32,128]{2,1,0:T(8,128)(2,1)} %get-tuple-element.7) | data formatting | bytes 524288 | tf_op jit(solution)/shard_map/stack | solution.py:195
  69.2 0.0 copy-done.2
  69.2 0.1 stack.13
  69.3 2.0 %pad_maximum_fusion = bf16[32,2,4096]{2,1,0:T(2,128)(2,1)} fusion(bf16[32,1,4096]{2,1,0:T(2,128)(2,1)S(1)} %stack.13, bf16[32,1,4096]{2,1,0:T(2,128)(2,1)S(1)} %stack.12), kind=kLoop, calls=%fused_computation | loop fusion | flops 1048576 | bytes 1048576 | tf_op jit(solution)/shard_map/stack | solution.py:195
Async XLA Ops:
  36.9 10.1 %copy-start = (bf16[32,32,128]{2,1,0:T(8,128)(2,1)S(1)}, bf16[32,32,128]{2,1,0:T(8,128)(2,1)}, u32[]{:S(2)}) copy-start(bf16[32,32,128]{2,1,0:T(8,128)(2,1)} %get-tuple-element.9.high_ref) | copy-start | bytes 786436
  36.9 12.0 %copy-start.1 = (bf16[32,32,128]{2,1,0:T(8,128)(2,1)S(1)}, bf16[32,32,128]{2,1,0:T(8,128)(2,1)}, u32[]{:S(2)}) copy-start(bf16[32,32,128]{2,1,0:T(8,128)(2,1)} %get-tuple-element.10.low_ref) | copy-start | bytes 786436
  36.9 20.4 %all-to-all-start.1 = ((f32[4,5,32,128]{3,2,1,0:T(8,128)}), f32[4,5,32,128]{3,2,1,0:T(8,128)S(1)}, u32[]{:S(2)}, u32[]{:S(2)}) async-start(f32[4,5,32,128]{3,2,1,0:T(8,128)} %column_sum.1), calls=%async_computation.1 | async-start | bytes 655360 | tf_op jit(solution)/shard_map/all_to_all | solution.py:184
  47.0 12.8 %collective-permute-start = (bf16[32,32,128]{2,1,0:T(8,128)(2,1)S(1)}, bf16[32,32,128]{2,1,0:T(8,128)(2,1)S(1)}, u32[]{:S(2)}, u32[]{:S(2)}) collective-permute-start(bf16[32,32,128]{2,1,0:T(8,128)(2,1)S(1)} %copy-done), channel_id=1, source_target_pairs={{0,32},{32,64},{64,96},{96,128},{128,160},{160,192},{192,224},{224... | collective-permute-start | bytes 786440 | tf_op jit(solution)/shard_map/ppermute | solution.py:158
  48.9 12.2 %collective-permute-start.1 = (bf16[32,32,128]{2,1,0:T(8,128)(2,1)S(1)}, bf16[32,32,128]{2,1,0:T(8,128)(2,1)S(1)}, u32[]{:S(2)}, u32[]{:S(2)}) collective-permute-start(bf16[32,32,128]{2,1,0:T(8,128)(2,1)S(1)} %copy-done.1), channel_id=1, source_target_pairs={{32,0},{64,32},{96,64},{128,96},{160,128},{192,160},{224,192},{256... | collective-permute-start | bytes 786440 | tf_op jit(solution)/shard_map/ppermute | solution.py:159
  59.7 1.4 %copy-start.3 = (bf16[32,32,128]{2,1,0:T(8,128)(2,1)}, bf16[32,32,128]{2,1,0:T(8,128)(2,1)S(1)}, u32[]{:S(2)}) copy-start(bf16[32,32,128]{2,1,0:T(8,128)(2,1)S(1)} %collective-permute-done.before_ref) | copy-start | bytes 786436
  61.1 0.7 copy-start.4
  67.2 2.0 %copy-start.2 = (bf16[32,32,128]{2,1,0:T(8,128)(2,1)S(1)}, bf16[32,32,128]{2,1,0:T(8,128)(2,1)}, u32[]{:S(2)}) copy-start(bf16[32,32,128]{2,1,0:T(8,128)(2,1)} %get-tuple-element.8) | copy-start | bytes 786436

commit v2 on v1

v2 whole, which is shorter than its diff:
```python
import jax
import jax.numpy as jnp
import numpy as np
from jax import lax
from jax.experimental import pallas as pl
from jax.experimental.pallas import tpu as pltpu
from jax.sharding import Mesh, PartitionSpec as P

NV = 1024
NODES = 33
ROWS = 32
LANES = 128
CELLS = (ROWS, LANES)
BOTH = (2 * ROWS, LANES)

speed_max = 4.0
time_step = 1.0 / 12.0
relax_coef = 0.1
center = 24.0
log2e = 1.4426950408889634

SIZES = (8, 2, 8, 2, 2)
NAMES = ("z", "xl", "y", "xh", "core")
GX = ("z", "xl")
VERT = ("y", "xh", "core")
QUAD = ("z", "xl", "xh", "core")

VMEM = pl.BlockSpec(memory_space=pltpu.VMEM)
SMEM = pl.BlockSpec(memory_space=pltpu.SMEM)
ANY = pl.BlockSpec(memory_space=pl.ANY)


def quad_place(z, xl, xh, core):
    return ((z % SIZES[0]) * 2 + xl) * 4 + xh * 2 + core


QUADS = [
    [quad_place(z, xl, xh, 0) for xl in range(2) for xh in range(2)] for z in range(SIZES[0])
] + [
    [quad_place(z + 1 - xl, xl, xh, 1) for xl in (1, 0) for xh in range(2)]
    for z in range(SIZES[0])
]


def node_table():
    steps = np.arange(NODES, dtype=np.float64) / (NODES - 1)
    return jnp.asarray(speed_max * np.cos(np.pi * steps), jnp.float32)


def small(mebibytes):
    return pltpu.CompilerParams(vmem_limit_bytes=mebibytes << 20)


def moments_kernel(index_ref, weight_ref, node_ref, dist_ref, out_ref, factor_ref, sums_ref):
    count = dist_ref.shape[0]
    for v in range(count):
        sx = node_ref[index_ref[0, v]]
        sy = node_ref[index_ref[1, v]]
        sz = node_ref[index_ref[2, v]]
        weight = weight_ref[v].astype(jnp.float32) * (512.0 / (32768.0 * NV))
        factor_ref[0, v] = weight
        factor_ref[1, v] = weight * sx
        factor_ref[2, v] = weight * sy
        factor_ref[3, v] = weight * sz
        factor_ref[4, v] = weight * (sx * sx + sy * sy + sz * sz - center)
    for part in range(2):
        rows = pl.ds(part * ROWS, ROWS)
        sums = [jnp.zeros(CELLS, jnp.float32) for _ in range(5)]
        for v in range(count):
            value = dist_ref[v, rows, :].astype(jnp.float32)
            sums = [total + factor_ref[comp, v] * value for comp, total in enumerate(sums)]
        for comp in range(5):
            sums_ref[comp, rows, :] = sums[comp]
    for plane in range(2):
        for comp in range(5):
            out_ref[plane, comp] = sums_ref[comp, pl.ds(plane, ROWS, stride=2), :]


def chip_kernel(plane_ref, both_ref, out_ref):
    plane = plane_ref[0]
    for comp in range(5):
        total = (both_ref[0, plane, comp] + both_ref[1, plane, comp]).astype(out_ref.dtype)
        for copy in range(out_ref.shape[0]):
            out_ref[copy, comp] = total


def split_kernel(after_ref, dist_ref, low_ref, high_ref, rows_ref):
    del after_ref

    def step(v, carry):
        slot = v & 3
        rows_ref[slot] = dist_ref[v].astype(jnp.float32)
        low_ref[v] = rows_ref[slot, pl.ds(0, ROWS, stride=2), :].astype(jnp.bfloat16)
        high_ref[v] = rows_ref[slot, pl.ds(1, ROWS, stride=2), :].astype(jnp.bfloat16)
        return carry

    lax.fori_loop(0, dist_ref.shape[0], step, 0, unroll=4)


def column_kernel(before_ref, after_ref, parts_ref, out_ref):
    del before_ref, after_ref
    for comp in range(5):
        total = parts_ref[0, comp].astype(jnp.float32)
        for part in range(1, parts_ref.shape[0]):
            total = total + parts_ref[part, comp].astype(jnp.float32)
        for copy in range(out_ref.shape[0]):
            out_ref[copy, comp] = total


def advance_kernel(side_ref, index_ref, node_ref, sums_ref, before_ref, dist_ref, after_ref, out_ref, own_ref, edge_params_ref, edge_ref):
    side = side_ref[0]
    for plane in range(4):
        half, pair = plane // 2, 2 * (plane % 2)
        half = half + (1 - side) * (1 - 2 * half)
        total = [sums_ref[half, pair, comp] + sums_ref[half, pair + 1, comp] for comp in range(5)]
        density = total[0]
        inverse = 1.0 / density
        flow = [total[comp] * inverse for comp in (1, 2, 3)]
        speed2 = flow[0] * flow[0] + flow[1] * flow[1] + flow[2] * flow[2]
        temper = (total[4] * inverse + center - speed2) * (1.0 / 3.0)
        root = jnp.sqrt(temper)
        rate = (time_step * relax_coef) * density * root
        scale = density * ((2.0 * np.pi) ** -1.5) / (temper * root)
        keep = 1.0 / (1.0 + rate)
        values = flow + [(-0.5 * log2e) / temper, scale * (rate * keep), keep]
        for comp in range(6):
            if plane in (1, 2):
                own_ref[comp, pl.ds(plane - 1, ROWS, stride=2), :] = values[comp]
            else:
                edge_params_ref[plane // 3, comp] = values[comp]
    lane = lax.broadcasted_iota(jnp.int32, BOTH, 1)
    parity = lax.broadcasted_iota(jnp.int32, BOTH, 0) & 1
    column = lane & 63
    upper = lane >> 6

    def relax(value, params, sx, sy, sz):
        dx = sx - params(0); dy = sy - params(1); dz = sz - params(2)
        spread = dx * dx + dy * dy + dz * dz
        equil = params(4) * jnp.exp2(spread * params(3))
        return (value.astype(jnp.float32) * params(5) + equil).astype(jnp.bfloat16).astype(jnp.float32)

    def step(v, carry):
        sx = node_ref[index_ref[0, v]]
        sy = node_ref[index_ref[1, v]]
        sz = node_ref[index_ref[2, v]]
        up_x, up_y, up_z = sx > 0.0, sy > 0.0, sz > 0.0
        ax, ay, az = (time_step * jnp.abs(s) for s in (sx, sy, sz))
        rest = 1.0 - (ax + ay + az)
        which = jnp.where(up_x, 0, 1)
        edge_value = jnp.where(up_x, before_ref[v].astype(jnp.float32), after_ref[v].astype(jnp.float32))
        edge = relax(edge_value, lambda c: edge_params_ref[which, c], sx, sy, sz)
        slot = lax.rem(v, edge_ref.shape[0])
        edge_ref[slot, pl.ds(0, ROWS, stride=2), :] = edge
        edge_ref[slot, pl.ds(1, ROWS, stride=2), :] = edge
        value = relax(dist_ref[v], lambda c: own_ref[c], sx, sy, sz)
        other = jnp.where(up_x, pltpu.roll(value, 1, 0), pltpu.roll(value, 63, 0))
        from_x = jnp.where(parity == which, edge_ref[slot], other)
        swapped = pltpu.roll(value, 64, 1)
        row = jnp.where(up_y, pltpu.roll(swapped, 2, 0), pltpu.roll(swapped, 62, 0))
        from_y = jnp.where(upper == jnp.where(up_y, 0, 1), row, swapped)
        near = pltpu.roll(value, jnp.where(up_z, 1, LANES - 1), 1)
        from_z = jnp.where(column == jnp.where(up_z, 0, 63), pltpu.roll(near, 64, 1), near)
        moved = rest * value + ax * from_x + ay * from_y + az * from_z
        out_ref[v] = moved.astype(jnp.bfloat16)
        return carry
    lax.fori_loop(0, dist_ref.shape[0], step, 0, unroll=2)


def shards(dist, vel_index, weight_int):
    count_v = dist.shape[0]
    nodes = node_table()
    side = lax.axis_index("xl")
    core = lax.axis_index("core")
    plane = jnp.reshape(1 ^ side ^ core, (1,)).astype(jnp.int32)
    side = jnp.reshape(side, (1,)).astype(jnp.int32)
    f32, bf16 = jnp.float32, jnp.bfloat16
    mixed = dist.reshape(count_v, 2, ROWS, LANES).transpose(0, 2, 1, 3).reshape((count_v,) + BOTH)

    partial_sums = pl.pallas_call(
        moments_kernel,
        out_shape=jax.ShapeDtypeStruct((2, 5) + CELLS, f32),
        in_specs=[SMEM, SMEM, SMEM, VMEM],
        out_specs=VMEM,
        scratch_shapes=[pltpu.SMEM((5, count_v), f32), pltpu.VMEM((5,) + BOTH, f32)],
        compiler_params=small(8),
        name="moments",
    )(vel_index, weight_int, nodes, mixed)
    both = lax.all_gather(partial_sums, "core")
    chip = pl.pallas_call(
        chip_kernel,
        out_shape=jax.ShapeDtypeStruct((SIZES[2], 5) + CELLS, bf16),
        in_specs=[SMEM, VMEM],
        out_specs=VMEM,
        compiler_params=small(4),
        name="chip_sum",
    )(plane, both)
    parts = lax.all_to_all(chip, "y", 0, 0)

    half = jax.ShapeDtypeStruct((count_v,) + CELLS, bf16)
    low, high = pl.pallas_call(
        split_kernel,
        out_shape=(half, half),
        in_specs=[ANY, VMEM],
        out_specs=(VMEM, VMEM),
        scratch_shapes=[pltpu.VMEM((4,) + BOTH, f32)],
        compiler_params=small(8),
        cost_estimate=pl.CostEstimate(flops=1 << 20, bytes_accessed=1 << 20, transcendentals=0),
        name="split_planes",
    )(chip, mixed)
    count = SIZES[0] * SIZES[1]
    forward = [(i, (i + 1) % count) for i in range(count)]
    backward = [(target, source) for source, target in forward]
    before = lax.ppermute(high, GX, forward)
    after = lax.ppermute(low, GX, backward)

    column = pl.pallas_call(
        column_kernel,
        out_shape=jax.ShapeDtypeStruct((4, 5) + CELLS, f32),
        in_specs=[ANY, ANY, VMEM],
        out_specs=VMEM,
        compiler_params=small(4),
        name="column_sum",
    )(before, after, parts)
    quad = lax.all_to_all(column, QUAD, 0, 0, axis_index_groups=QUADS)
    sums = lax.all_gather(quad, "core")
    out = pl.pallas_call(
        advance_kernel,
        out_shape=jax.ShapeDtypeStruct(mixed.shape, bf16),
        in_specs=[SMEM, SMEM, SMEM, VMEM, VMEM, VMEM, VMEM],
        out_specs=VMEM,
        scratch_shapes=[
            pltpu.VMEM((6,) + BOTH, f32),
            pltpu.VMEM((2, 6) + CELLS, f32),
            pltpu.VMEM((4,) + BOTH, f32),
        ],
        compiler_params=small(16),
        name="advance",
    )(side, vel_index, nodes, sums, before, mixed, after)
    return out.reshape(count_v, ROWS, 2, LANES).transpose(0, 2, 1, 3).reshape(dist.shape)


def solution(mesh):
    parts = Mesh(mesh.devices.reshape(SIZES), NAMES)
    return jax.shard_map(
        shards,
        mesh=parts,
        in_specs=(P(VERT, GX, None), P(None, VERT), P(VERT)),
        out_specs=P(VERT, GX, None),
        check_vma=False,
    )
```

time: 72 us -> 53.9 us (0.75)
  blocking collectives: 31.2 us -> 24.7 us
  Pallas kernels: 11.1 us -> 6.78 us
  local copies, waits for them, and re-layouts: 5.12 us -> 1.73 us
  starting transfers between devices: 17.5 us -> 14.9 us
  other arithmetic: 1.99 us -> 0 us
  waiting for transfers between devices: 4.36 us -> 5.33 us
    all_to_all x1, starting transfers between devices: 10.1 us -> 3.43 us  [shards(): parts = lax.all_to_all(chip, 'y', 0, 0)]
    ppermute x1, waiting for transfers between devices: 0.01 us -> 4.17 us  [shards(): before = lax.ppermute(high, GX, forward)]
    ppermute x1, starting transfers between devices: 5.47 us -> 9.6 us  [shards(): after = lax.ppermute(low, GX, backward)]
    all_to_all x1, blocking collectives: 17.8 us -> 13.9 us  [shards(): quad = lax.all_to_all(column, QUAD, 0, 0, axis_index_groups=QUADS)]
    all_to_all x1, waiting for transfers between devices: 2.96 us -> 0.01 us  [shards(): parts = lax.all_to_all(chip, 'y', 0, 0)]
    all_gather x1, blocking collectives: 11 us -> 8.55 us  [shards(): both = lax.all_gather(partial_sums, 'core')]
    another operation x2 -> x0, local copies, waits for them, and re-layouts: 2.13 us -> none  [shards(): return jnp.stack([out_low, out_high], axis=1).reshape(dist.shape)]
    another operation x1 -> x0, other arithmetic: 1.99 us -> none  [shards(): return jnp.stack([out_low, out_high], axis=1).reshape(dist.shape)]
  transfers between devices with their start and end apart: 3 -> 3, of which waited for: 2 -> 2; matrix products, arithmetic and copies ran while one was open for 0% -> 0% of each run, Pallas kernels for 0% -> 1%
where the time goes in v2:
time: 53.9 us; the launch traced here: 53.5 us
  blocking collectives  24.7 us (46%)
  starting transfers between devices  14.9 us (28%)
  Pallas kernels  6.78 us (13%)
  waiting for transfers between devices  5.33 us (10%)
  local copies, waits for them, and re-layouts  1.73 us (3%)
    all_to_all x1, blocking collectives, shards(): quad = lax.all_to_all(column, QUAD, 0, 0, axis_index_groups=QUADS)  13.9 us
    ppermute x1, starting transfers between devices, shards(): after = lax.ppermute(low, GX, backward)  9.6 us
    all_gather x1, blocking collectives, shards(): both = lax.all_gather(partial_sums, 'core')  8.55 us
    pallas_call x1, Pallas kernels, shards(): pl.pallas_call(advance_kernel, out_shape=jax.ShapeDtypeStruct(mixed.shape...  4.57 us
    ppermute x1, waiting for transfers between devices, shards(): before = lax.ppermute(high, GX, forward)  4.17 us
    all_to_all x1, starting transfers between devices, shards(): parts = lax.all_to_all(chip, 'y', 0, 0)  3.43 us
    all_gather x1, blocking collectives, shards(): sums = lax.all_gather(quad, 'core')  2.26 us
    ppermute x1, starting transfers between devices, shards(): before = lax.ppermute(high, GX, forward)  1.91 us
  transfers between devices with their start and end apart: 3, of which 2 were waited for; matrix products, arithmetic and copies ran while one was open for 0% of the time, Pallas kernels for 1%

profile of v2, /device:TPU:1, one launch (start us, length us, event | category | flops | bytes accessed | tf_op | source)
XLA Modules:
  0.0 53.5 jit_solution(2710327372798799023)
XLA Ops:
  0.0 0.0 copy-start.2
  0.0 0.0 copy-start.3
  0.0 0.0 copy-start.4
  0.0 0.7 %copy-done.2 = s32[3,32]{1,0:T(4,128)S(1)} copy-done((s32[3,32]{1,0:T(4,128)S(1)}, s32[3,32]{1,0:T(4,128)}, u32[]{:S(2)}) %copy-start.2) | copy-done | bytes 408
  0.7 0.0 copy-done.3
  0.7 0.0 copy-done.4
  0.7 0.0 copy-start
  0.7 1.0 %copy-done = bf16[32,2,4096]{2,1,0:T(2,128)(2,1)S(1)} copy-done((bf16[32,2,4096]{2,1,0:T(2,128)(2,1)S(1)}, bf16[32,2,4096]{2,1,0:T(2,128)(2,1)}, u32[]{:S(2)}) %copy-start) | copy-done | bytes 524312
  1.7 1.0 %moments.1 = f32[2,5,32,128]{3,2,1,0:T(8,128)S(1)} custom-call(s32[3,32]{1,0:T(4,128)S(1)} %copy-done.2, s32[32]{0:T(128)S(1)} %copy-done.4, f32[33]{0:T(128)S(1)} %copy-done.3, bf16[32,64,128]{2,1,0:T(8,128)(2,1)S(1)} %bitcast.14), custom_call_target="tpu_custom_call" | custom-call | tf_op jit(solution)/shard_map/moments/pallas_call | solution.py:179
  2.7 8.6 %all-gather = f32[4,5,32,128]{3,2,1,0:T(8,128)S(1)} all-gather(f32[2,5,32,128]{3,2,1,0:T(8,128)S(1)} %moments.1), channel_id=2, replica_groups=mesh['z'=8,'xl'=2,'y'=8,'xh'=2,'core'=2] {'core'}, dimensions={0}, use_global_device_ids=true | all-gather | bytes 491520 | tf_op jit(solution)/shard_map/all_gather | solution.py:188
  11.3 0.0 copy-start.1
  11.3 0.7 %chip_sum.1.after_ref = bf16[8,5,32,128]{3,2,1,0:T(8,128)(2,1)} custom-call(s32[1]{0:T(128)} %bitcast.1.plane_ref, f32[2,2,5,32,128]{4,3,2,1,0:T(8,128)S(1)} %bitcast.18), custom_call_target="tpu_custom_call" | custom-call | tf_op jit(solution)/shard_map/chip_sum/pallas_call | solution.py:189
  12.0 3.4 %all-to-all-start = ((bf16[8,5,32,128]{3,2,1,0:T(8,128)(2,1)}), bf16[8,5,32,128]{3,2,1,0:T(8,128)(2,1)S(1)}, u32[]{:S(2)}, u32[]{:S(2)}) async-start(bf16[8,5,32,128]{3,2,1,0:T(8,128)(2,1)} %chip_sum.1.after_ref), calls=%async_computation | async-start | bytes 655360 | tf_op jit(solution)/shard_map/all_to_all | solution.py:197
  15.5 0.0 copy-done.1
  15.5 0.4 split_planes.1
  15.9 1.9 %collective-permute-start = (bf16[32,32,128]{2,1,0:T(8,128)(2,1)S(1)}, bf16[32,32,128]{2,1,0:T(8,128)(2,1)S(1)}, u32[]{:S(2)}, u32[]{:S(2)}) collective-permute-start(bf16[32,32,128]{2,1,0:T(8,128)(2,1)S(1)} %get-tuple-element.7), channel_id=1, source_target_pairs={{0,32},{32,64},{64,96},{96,128},{128,160},{160,192},{192,224},{224... | collective-permute-start | bytes 786440 | tf_op jit(solution)/shard_map/ppermute | solution.py:213
  17.8 9.6 %collective-permute-start.1 = (bf16[32,32,128]{2,1,0:T(8,128)(2,1)S(1)}, bf16[32,32,128]{2,1,0:T(8,128)(2,1)S(1)}, u32[]{:S(2)}, u32[]{:S(2)}) collective-permute-start(bf16[32,32,128]{2,1,0:T(8,128)(2,1)S(1)} %get-tuple-element.8), channel_id=1, source_target_pairs={{32,0},{64,32},{96,64},{128,96},{160,128},{192,160},{224,192},{256... | collective-permute-start | bytes 786440 | tf_op jit(solution)/shard_map/ppermute | solution.py:214
  27.4 4.2 %collective-permute-done.before_ref = bf16[32,32,128]{2,1,0:T(8,128)(2,1)S(1)} collective-permute-done((bf16[32,32,128]{2,1,0:T(8,128)(2,1)S(1)}, bf16[32,32,128]{2,1,0:T(8,128)(2,1)S(1)}, u32[]{:S(2)}, u32[]{:S(2)}) %collective-permute-start) | collective-permute-done | bytes 262176 | tf_op jit(solution)/shard_map/ppermute | solution.py:213
  31.6 1.2 %collective-permute-done.1.after_ref = bf16[32,32,128]{2,1,0:T(8,128)(2,1)S(1)} collective-permute-done((bf16[32,32,128]{2,1,0:T(8,128)(2,1)S(1)}, bf16[32,32,128]{2,1,0:T(8,128)(2,1)S(1)}, u32[]{:S(2)}, u32[]{:S(2)}) %collective-permute-start.1) | collective-permute-done | bytes 262176 | tf_op jit(solution)/shard_map/ppermute | solution.py:214
  32.7 0.0 all-to-all-done.parts_ref
  32.8 13.9 %all_to_all.10 = f32[4,5,32,128]{3,2,1,0:T(8,128)S(1)} all-to-all(f32[4,5,32,128]{3,2,1,0:T(8,128)S(1)} %column_sum.1), channel_id=1, replica_groups={{0,2,32,34},{64,66,96,98},{128,130,160,162},{192,194,224,226},{256,258,..., dimensions={0} | all-to-all | bytes 655360 | tf_op jit(solution)/shard_map/all_to_all | solution.py:224
  46.7 2.3 %all-gather.1 = f32[8,5,32,128]{3,2,1,0:T(8,128)S(1)} all-gather(f32[4,5,32,128]{3,2,1,0:T(8,128)S(1)} %all_to_all.10), channel_id=3, replica_groups=mesh['z'=8,'xl'=2,'y'=8,'xh'=2,'core'=2] {'core'}, dimensions={0}, use_global_device_ids=true | all-gather | bytes 983040 | tf_op jit(solution)/shard_map/all_gather | solution.py:225
  48.9 4.6 %advance.1 = bf16[32,64,128]{2,1,0:T(8,128)(2,1)} custom-call(s32[1]{0:T(128)} %bitcast.side_ref, s32[3,32]{1,0:T(4,128)S(1)} %copy-done.2, f32[33]{0:T(128)S(1)} %copy-done.3, f32[2,4,5,32,128]{4,3,2,1,0:T(8,128)S(1)} %bitcast.17, bf16[32,32,128]{2,1,0:T(8,128)(2,1)S(1)} %collective-permute-done.before_ref, bf16[32,64,128]{2,1,0:T(8,128)(2,1)S(1)} %bitcast.16, ...), custom_call_target="tpu_custom_call" | custom-call | tf_op jit(solution)/shard_map/advance/pallas_call | solution.py:226
  (1 shorter events, 0.0 us)
Async XLA Ops:
  0.0 0.7 %copy-start.2 = (s32[3,32]{1,0:T(4,128)S(1)}, s32[3,32]{1,0:T(4,128)}, u32[]{:S(2)}) copy-start(s32[3,32]{1,0:T(4,128)} %index_ref.3) | copy-start | bytes 1156
  0.0 0.7 %copy-start.3 = (f32[33]{0:T(128)S(1)}, f32[33]{0:T(128)}, u32[]{:S(2)}) copy-start(f32[33]{0:T(128)} %constant.12.clone.node_ref) | copy-start | bytes 400
  0.0 0.7 %copy-start.4 = (s32[32]{0:T(128)S(1)}, s32[32]{0:T(128)}, u32[]{:S(2)}) copy-start(s32[32]{0:T(128)} %weight_ref.1) | copy-start | bytes 388
  0.7 1.0 %copy-start = (bf16[32,2,4096]{2,1,0:T(2,128)(2,1)S(1)}, bf16[32,2,4096]{2,1,0:T(2,128)(2,1)}, u32[]{:S(2)}) copy-start(bf16[32,2,4096]{2,1,0:T(2,128)(2,1)} %param.4) | copy-start | bytes 1572868
  11.3 4.2 %copy-start.1 = (bf16[32,2,4096]{2,1,0:T(2,128)(2,1)S(1)}, bf16[32,2,4096]{2,1,0:T(2,128)(2,1)}, u32[]{:S(2)}) copy-start(bf16[32,2,4096]{2,1,0:T(2,128)(2,1)} %param.4) | copy-start | bytes 1572868
  12.0 20.7 %all-to-all-start = ((bf16[8,5,32,128]{3,2,1,0:T(8,128)(2,1)}), bf16[8,5,32,128]{3,2,1,0:T(8,128)(2,1)S(1)}, u32[]{:S(2)}, u32[]{:S(2)}) async-start(bf16[8,5,32,128]{3,2,1,0:T(8,128)(2,1)} %chip_sum.1.after_ref), calls=%async_computation | async-start | bytes 655360 | tf_op jit(solution)/shard_map/all_to_all | solution.py:197
  15.9 15.7 %collective-permute-start = (bf16[32,32,128]{2,1,0:T(8,128)(2,1)S(1)}, bf16[32,32,128]{2,1,0:T(8,128)(2,1)S(1)}, u32[]{:S(2)}, u32[]{:S(2)}) collective-permute-start(bf16[32,32,128]{2,1,0:T(8,128)(2,1)S(1)} %get-tuple-element.7), channel_id=1, source_target_pairs={{0,32},{32,64},{64,96},{96,128},{128,160},{160,192},{192,224},{224... | collective-permute-start | bytes 786440 | tf_op jit(solution)/shard_map/ppermute | solution.py:213
  17.8 14.9 %collective-permute-start.1 = (bf16[32,32,128]{2,1,0:T(8,128)(2,1)S(1)}, bf16[32,32,128]{2,1,0:T(8,128)(2,1)S(1)}, u32[]{:S(2)}, u32[]{:S(2)}) collective-permute-start(bf16[32,32,128]{2,1,0:T(8,128)(2,1)S(1)} %get-tuple-element.8), channel_id=1, source_target_pairs={{32,0},{64,32},{96,64},{128,96},{160,128},{192,160},{224,192},{256... | collective-permute-start | bytes 786440 | tf_op jit(solution)/shard_map/ppermute | solution.py:214

commit v3 on v2

v3 whole, which is shorter than its diff:
```python
import jax
import jax.numpy as jnp
import numpy as np
from jax import lax
from jax.experimental import pallas as pl
from jax.experimental.pallas import tpu as pltpu
from jax.sharding import Mesh, PartitionSpec as P

NV = 1024
NODES = 33
ROWS = 32
LANES = 128
CELLS = (ROWS, LANES)
BOTH = (2 * ROWS, LANES)

speed_max = 4.0
time_step = 1.0 / 12.0
relax_coef = 0.1
center = 24.0
log2e = 1.4426950408889634

SIZES = (8, 2, 8, 2, 2)
NAMES = ("z", "xl", "y", "xh", "core")
GX = ("z", "xl")
VERT = ("y", "xh", "core")

VMEM = pl.BlockSpec(memory_space=pltpu.VMEM)
SMEM = pl.BlockSpec(memory_space=pltpu.SMEM)
ANY = pl.BlockSpec(memory_space=pl.ANY)
HBM = pl.BlockSpec(memory_space=pltpu.HBM)


OWNERS = SIZES[2] * SIZES[3]
SHARE = ROWS // OWNERS
CHUNK = 16


def place(z, xl, y, xh, core):
    return ((((z % SIZES[0]) * 2 + xl) * SIZES[2] + y) * 2 + xh) * 2 + core


PAIRS = [[(z, 0, 0), (z, 1, 0)] for z in range(SIZES[0])] + [
    [(z, 1, 1), (z + 1, 0, 1)] for z in range(SIZES[0])
]
GROUPS = [
    [place(z, xl, y, xh, core) for z, xl, core in pair for y in range(SIZES[2]) for xh in range(2)]
    for pair in PAIRS
]
NODE_SPEEDS = [float(speed_max * np.cos(np.pi * j / (NODES - 1))) for j in range(NODES)]


def fill_nodes(node_ref):
    for j, speed in enumerate(NODE_SPEEDS):
        node_ref[j] = jnp.float32(speed)


def small(mebibytes):
    return pltpu.CompilerParams(vmem_limit_bytes=mebibytes << 20)


def moments_kernel(
    side_ref, index_hbm, weight_hbm, dist_hbm, out_ref,
    index_ref, weight_ref, node_ref, factor_ref, dist_ref, sums_ref, chunk_ref, small_sems, sems,
):
    count = dist_ref.shape[0]
    half = count // 2
    pieces = []
    for part in range(2):
        for k in range(2):
            where = (pl.ds(k * half, half), pl.ds(part * ROWS, ROWS))
            pieces.append(pltpu.make_async_copy(dist_hbm.at[where], dist_ref.at[where], sems.at[2 * part + k]))
    tables = [
        pltpu.make_async_copy(index_hbm, index_ref, small_sems.at[0]),
        pltpu.make_async_copy(weight_hbm, weight_ref, small_sems.at[1]),
    ]
    for copy in tables + pieces:
        copy.start()
    fill_nodes(node_ref)
    for copy in tables:
        copy.wait()
    for v in range(count):
        sx = node_ref[index_ref[0, v]]
        sy = node_ref[index_ref[1, v]]
        sz = node_ref[index_ref[2, v]]
        weight = weight_ref[v].astype(jnp.float32) * (512.0 / (32768.0 * NV))
        factor_ref[0, v] = weight
        factor_ref[1, v] = weight * sx
        factor_ref[2, v] = weight * sy
        factor_ref[3, v] = weight * sz
        factor_ref[4, v] = weight * (sx * sx + sy * sy + sz * sz - center)
    for part in range(2):
        rows = pl.ds(part * ROWS, ROWS)
        sums = [jnp.zeros(CELLS, jnp.float32) for _ in range(5)]
        for v in range(count):
            if v % half == 0:
                pieces[2 * part + v // half].wait()
            value = dist_ref[v, rows, :].astype(jnp.float32)
            sums = [total + factor_ref[comp, v] * value for comp, total in enumerate(sums)]
        for comp in range(5):
            sums_ref[comp, rows, :] = sums[comp]
    side = side_ref[0]
    for core in range(2):
        plane = 1 - core + side * (2 * core - 1)
        for comp in range(5):
            for r in range(SHARE):
                picked = sums_ref[comp, pl.ds(SHARE * r + plane, OWNERS, stride=2 * SHARE), :]
                chunk_ref[core, pl.ds(SHARE * comp + r, OWNERS, stride=CHUNK), :] = picked
        for r in range(5 * SHARE, CHUNK):
            chunk_ref[core, pl.ds(r, OWNERS, stride=CHUNK), :] = jnp.zeros((OWNERS, LANES), jnp.float32)
        for e in range(OWNERS):
            out_ref[2 * e + core] = chunk_ref[core, pl.ds(CHUNK * e, CHUNK), :].astype(out_ref.dtype)


def split_kernel(token_ref, dist_ref, low_ref, high_a_ref, high_b_ref, rows_ref):
    del token_ref
    half = high_a_ref.shape[0]

    def step(v, carry):
        for k, high_ref in enumerate((high_a_ref, high_b_ref)):
            slot, at = 2 * (v & 1) + k, v + k * half
            rows_ref[slot] = dist_ref[at].astype(jnp.float32)
            low_ref[at] = rows_ref[slot, pl.ds(0, ROWS, stride=2), :].astype(jnp.bfloat16)
            high_ref[v] = rows_ref[slot, pl.ds(1, ROWS, stride=2), :].astype(jnp.bfloat16)
        return carry

    lax.fori_loop(0, half, step, 0, unroll=2)


def owner_kernel(token_a_ref, token_b_ref, parts_ref, out_ref):
    del token_a_ref, token_b_ref
    total = parts_ref[0].astype(jnp.float32)
    for part in range(1, parts_ref.shape[0]):
        total = total + parts_ref[part].astype(jnp.float32)
    for copy in range(out_ref.shape[0]):
        out_ref[copy] = total


def advance_kernel(
    side_ref, index_ref, sums_ref, before_ref, dist_ref, after_ref, out_ref,
    node_ref, own_ref, edge_params_ref, edge_ref,
):
    fill_nodes(node_ref)
    side = side_ref[0]
    for plane, r in [(plane, r) for plane in range(4) for r in range(SHARE)]:
        half, pair = plane // 2, plane % 2
        half = half + (1 - side) * (1 - 2 * half)
        first = pair * OWNERS * CHUNK + r
        total = [
            sums_ref[half, pl.ds(first + SHARE * comp, OWNERS, stride=CHUNK), :] for comp in range(5)
        ]
        density = total[0]
        inverse = 1.0 / density
        flow = [total[comp] * inverse for comp in (1, 2, 3)]
        speed2 = flow[0] * flow[0] + flow[1] * flow[1] + flow[2] * flow[2]
        temper = (total[4] * inverse + center - speed2) * (1.0 / 3.0)
        root = jnp.sqrt(temper)
        rate = (time_step * relax_coef) * density * root
        scale = density * ((2.0 * np.pi) ** -1.5) / (temper * root)
        keep = 1.0 / (1.0 + rate)
        values = flow + [(-0.5 * log2e) / temper, scale * (rate * keep), keep]
        for comp in range(6):
            if plane in (1, 2):
                rows = pl.ds(2 * r + plane - 1, OWNERS, stride=2 * SHARE)
                own_ref[comp, rows, :] = values[comp]
            else:
                edge_params_ref[plane // 3, comp, pl.ds(r, OWNERS, stride=SHARE), :] = values[comp]
    lane = lax.broadcasted_iota(jnp.int32, BOTH, 1)
    parity = lax.broadcasted_iota(jnp.int32, BOTH, 0) & 1
    column = lane & 63
    upper = lane >> 6

    def relax(value, params, sx, sy, sz):
        dx = sx - params(0); dy = sy - params(1); dz = sz - params(2)
        spread = dx * dx + dy * dy + dz * dz
        equil = params(4) * jnp.exp2(spread * params(3))
        return (value.astype(jnp.float32) * params(5) + equil).astype(jnp.bfloat16).astype(jnp.float32)

    def step(v, carry):
        sx = node_ref[index_ref[0, v]]
        sy = node_ref[index_ref[1, v]]
        sz = node_ref[index_ref[2, v]]
        up_x, up_y, up_z = sx > 0.0, sy > 0.0, sz > 0.0
        ax, ay, az = (time_step * jnp.abs(s) for s in (sx, sy, sz))
        rest = 1.0 - (ax + ay + az)
        which = jnp.where(up_x, 0, 1)
        edge_value = jnp.where(up_x, before_ref[v].astype(jnp.float32), after_ref[v].astype(jnp.float32))
        edge = relax(edge_value, lambda c: edge_params_ref[which, c], sx, sy, sz)
        slot = lax.rem(v, edge_ref.shape[0])
        edge_ref[slot, pl.ds(0, ROWS, stride=2), :] = edge
        edge_ref[slot, pl.ds(1, ROWS, stride=2), :] = edge
        value = relax(dist_ref[v], lambda c: own_ref[c], sx, sy, sz)
        other = jnp.where(up_x, pltpu.roll(value, 1, 0), pltpu.roll(value, 63, 0))
        from_x = jnp.where(parity == which, edge_ref[slot], other)
        swapped = pltpu.roll(value, 64, 1)
        row = jnp.where(up_y, pltpu.roll(swapped, 2, 0), pltpu.roll(swapped, 62, 0))
        from_y = jnp.where(upper == jnp.where(up_y, 0, 1), row, swapped)
        near = pltpu.roll(value, jnp.where(up_z, 1, LANES - 1), 1)
        from_z = jnp.where(column == jnp.where(up_z, 0, 63), pltpu.roll(near, 64, 1), near)
        moved = rest * value + ax * from_x + ay * from_y + az * from_z
        out_ref[v] = moved.astype(jnp.bfloat16)
        return carry
    lax.fori_loop(0, dist_ref.shape[0], step, 0, unroll=2)


def shards(dist, vel_index, weight_int):
    count_v = dist.shape[0]
    side = jnp.reshape(lax.axis_index("xl"), (1,)).astype(jnp.int32)
    f32, bf16 = jnp.float32, jnp.bfloat16
    mixed = dist.reshape(count_v, 2, ROWS, LANES).transpose(0, 2, 1, 3).reshape((count_v,) + BOTH)

    chunks = pl.pallas_call(
        moments_kernel,
        out_shape=jax.ShapeDtypeStruct((2 * OWNERS, CHUNK, LANES), bf16),
        in_specs=[SMEM, HBM, HBM, HBM],
        out_specs=VMEM,
        scratch_shapes=[
            pltpu.SMEM(vel_index.shape, jnp.int32),
            pltpu.SMEM(weight_int.shape, jnp.int32),
            pltpu.SMEM((NODES,), f32),
            pltpu.SMEM((5, count_v), f32),
            pltpu.VMEM(mixed.shape, bf16),
            pltpu.VMEM((5,) + BOTH, f32),
            pltpu.VMEM((2, OWNERS * CHUNK, LANES), f32),
            pltpu.SemaphoreType.DMA((2,)),
            pltpu.SemaphoreType.DMA((4,)),
        ],
        compiler_params=small(56),
        name="moments",
    )(side, vel_index, weight_int, mixed)
    parts = lax.all_to_all(chunks, VERT, 0, 0)

    whole = jax.ShapeDtypeStruct((count_v,) + CELLS, bf16)
    half = jax.ShapeDtypeStruct((count_v // 2,) + CELLS, bf16)
    low, high_a, high_b = pl.pallas_call(
        split_kernel,
        out_shape=(whole, half, half),
        in_specs=[ANY, VMEM],
        out_specs=(VMEM, VMEM, VMEM),
        scratch_shapes=[pltpu.VMEM((4,) + BOTH, f32)],
        compiler_params=small(8),
        cost_estimate=pl.CostEstimate(flops=1 << 33, bytes_accessed=1 << 25, transcendentals=0),
        name="split_planes",
    )(chunks, mixed)
    count = SIZES[0] * SIZES[1]
    forward = [(i, (i + 1) % count) for i in range(count)]
    backward = [(target, source) for source, target in forward]
    before_a = lax.ppermute(high_a, GX, forward)
    before_b = lax.ppermute(high_b, GX, forward)
    after = lax.ppermute(low, GX, backward)

    owned = pl.pallas_call(
        owner_kernel,
        out_shape=jax.ShapeDtypeStruct((2 * OWNERS, CHUNK, LANES), f32),
        in_specs=[ANY, ANY, VMEM],
        out_specs=VMEM,
        compiler_params=small(4),
        name="owner_sum",
    )(before_a, before_b, parts)
    before = jnp.concatenate([before_a, before_b])
    gathered = lax.all_to_all(owned, NAMES, 0, 0, axis_index_groups=GROUPS)
    sums = lax.all_gather(gathered.reshape(2 * OWNERS * CHUNK, LANES), "core")
    out = pl.pallas_call(
        advance_kernel,
        out_shape=jax.ShapeDtypeStruct(mixed.shape, bf16),
        in_specs=[SMEM, SMEM, VMEM, VMEM, VMEM, VMEM],
        out_specs=VMEM,
        scratch_shapes=[
            pltpu.SMEM((NODES,), f32),
            pltpu.VMEM((6,) + BOTH, f32),
            pltpu.VMEM((2, 6) + CELLS, f32),
            pltpu.VMEM((4,) + BOTH, f32),
        ],
        compiler_params=small(16),
        name="advance",
    )(side, vel_index, sums, before, mixed, after)
    return out.reshape(count_v, ROWS, 2, LANES).transpose(0, 2, 1, 3).reshape(dist.shape)


def solution(mesh):
    parts = Mesh(mesh.devices.reshape(SIZES), NAMES)
    return jax.shard_map(
        shards,
        mesh=parts,
        in_specs=(P(VERT, GX, None), P(None, VERT), P(VERT)),
        out_specs=P(VERT, GX, None),
        check_vma=False,
    )
```

time: 53.9 us -> 63.3 us (1.17)
  blocking collectives: 24.7 us -> 4.36 us
  starting transfers between devices: 14.9 us -> 32 us
  waiting for transfers between devices: 5.33 us -> 18.5 us
  local copies, waits for them, and re-layouts: 1.73 us -> 0.01 us
  Pallas kernels: 6.78 us -> 7.97 us
    all_to_all x1 -> x2, starting transfers between devices: 3.43 us -> 22.8 us  [the longest x1 11.4 us: shards(): gathered = lax.all_to_all(owned, NAMES, 0, 0, axis_index_groups=GROUPS)]
    all_to_all x1 -> x0, blocking collectives: 13.9 us -> none  [shards(): quad = lax.all_to_all(column, QUAD, 0, 0, axis_index_groups=QUADS)]
    all_to_all x1 -> x2, waiting for transfers between devices: 0.01 us -> 8.42 us  [the longest x1 8.41 us: shards(): gathered = lax.all_to_all(owned, NAMES, 0, 0, axis_index_groups=GROUPS)]
    ppermute x1, starting transfers between devices: 9.6 us -> 2.14 us  [shards(): after = lax.ppermute(low, GX, backward)]
    all_gather x2 -> x1, blocking collectives: 10.8 us -> 4.36 us  [shards(): sums = lax.all_gather(gathered.reshape(2 * OWNERS * CHUNK, LANES), 'core')]
    ppermute x1 -> x2, waiting for transfers between devices: 4.17 us -> 10.1 us  [the longest x1 7.3 us: shards(): before_a = lax.ppermute(high_a, GX, forward)]
    ppermute x1 -> x2, starting transfers between devices: 1.91 us -> 7.09 us  [the longest x1 4.87 us: shards(): before_b = lax.ppermute(high_b, GX, forward)]
    unnamed x10 -> x6, local copies, waits for them, and re-layouts: 1.73 us -> 0.01 us
  transfers between devices with their start and end apart: 3 -> 5, of which waited for: 2 -> 3; matrix products, arithmetic and copies ran while one was open for 0% -> 0% of each run, Pallas kernels for 1% -> 0%
where the time goes in v3:
time: 63.3 us; the launch traced here: 63 us
  starting transfers between devices  32 us (51%)
  waiting for transfers between devices  18.5 us (29%)
  Pallas kernels  7.97 us (13%)
  blocking collectives  4.36 us (7%)
    all_to_all x1, starting transfers between devices, shards(): gathered = lax.all_to_all(owned, NAMES, 0, 0, axis_index_groups=GROUPS)  11.4 us
    all_to_all x1, starting transfers between devices, shards(): parts = lax.all_to_all(chunks, VERT, 0, 0)  11.4 us
    all_to_all x1, waiting for transfers between devices, shards(): gathered = lax.all_to_all(owned, NAMES, 0, 0, axis_index_groups=GROUPS)  8.41 us
    ppermute x1, waiting for transfers between devices, shards(): before_a = lax.ppermute(high_a, GX, forward)  7.3 us
    ppermute x1, starting transfers between devices, shards(): before_b = lax.ppermute(high_b, GX, forward)  4.87 us
    pallas_call x1, Pallas kernels, shards(): pl.pallas_call(advance_kernel, out_shape=jax.ShapeDtypeStruct(mixed.shape...  4.69 us
    all_gather x1, blocking collectives, shards(): sums = lax.all_gather(gathered.reshape(2 * OWNERS * CHUNK, LANES), 'core')  4.36 us
    ppermute x1, waiting for transfers between devices, shards(): before_b = lax.ppermute(high_b, GX, forward)  2.81 us
  transfers between devices with their start and end apart: 5, of which 3 were waited for; matrix products, arithmetic and copies ran while one was open for 0% of the time, Pallas kernels for 0%

profile of v3, /device:TPU:1, one launch (start us, length us, event | category | flops | bytes accessed | tf_op | source)
XLA Modules:
  0.0 63.0 jit_solution(12763095248221487052)
XLA Ops:
  0.0 0.0 copy-start
  0.0 2.2 %moments.1.token_ref = bf16[32,16,128]{2,1,0:T(8,128)(2,1)} custom-call(s32[1]{0:T(128)} %bitcast.side_ref, s32[3,32]{1,0:T(4,128)} %index_ref.1, s32[32]{0:T(128)} %weight_hbm.1, bf16[32,64,128]{2,1,0:T(8,128)(2,1)} %bitcast.12), custom_call_target="tpu_custom_call" | custom-call | tf_op jit(solution)/shard_map/moments/pallas_call | solution.py:211
  2.2 0.0 copy-start.1
  2.3 11.4 %all-to-all-start = ((bf16[32,16,128]{2,1,0:T(8,128)(2,1)}), bf16[32,16,128]{2,1,0:T(8,128)(2,1)S(1)}, u32[]{:S(2)}, u32[]{:S(2)}) async-start(bf16[32,16,128]{2,1,0:T(8,128)(2,1)} %moments.1.token_ref), calls=%async_computation | async-start | bytes 262144 | tf_op jit(solution)/shard_map/all_to_all | solution.py:230
  13.6 0.0 copy-done
  13.6 0.0 copy-done.1
  13.6 0.3 split_planes.1
  13.9 2.2 %collective-permute-start = (bf16[16,32,128]{2,1,0:T(8,128)(2,1)S(1)}, bf16[16,32,128]{2,1,0:T(8,128)(2,1)S(1)}, u32[]{:S(2)}, u32[]{:S(2)}) collective-permute-start(bf16[16,32,128]{2,1,0:T(8,128)(2,1)S(1)} %get-tuple-element.8), channel_id=1, source_target_pairs={{0,32},{32,64},{64,96},{96,128},{128,160},{160,192},{192,224},{224... | collective-permute-start | bytes 393224 | tf_op jit(solution)/shard_map/ppermute | solution.py:247
  16.2 4.9 %collective-permute-start.1 = (bf16[16,32,128]{2,1,0:T(8,128)(2,1)S(1)}, bf16[16,32,128]{2,1,0:T(8,128)(2,1)S(1)}, u32[]{:S(2)}, u32[]{:S(2)}) collective-permute-start(bf16[16,32,128]{2,1,0:T(8,128)(2,1)S(1)} %get-tuple-element.9), channel_id=1, source_target_pairs={{0,32},{32,64},{64,96},{96,128},{128,160},{160,192},{192,224},{224... | collective-permute-start | bytes 393224 | tf_op jit(solution)/shard_map/ppermute | solution.py:248
  21.0 7.3 %collective-permute-done.token_a_ref = bf16[16,32,128]{2,1,0:T(8,128)(2,1)S(1)} collective-permute-done((bf16[16,32,128]{2,1,0:T(8,128)(2,1)S(1)}, bf16[16,32,128]{2,1,0:T(8,128)(2,1)S(1)}, u32[]{:S(2)}, u32[]{:S(2)}) %collective-permute-start) | collective-permute-done | bytes 131104 | tf_op jit(solution)/shard_map/ppermute | solution.py:247
  28.3 2.8 %collective-permute-done.1.token_b_ref = bf16[16,32,128]{2,1,0:T(8,128)(2,1)S(1)} collective-permute-done((bf16[16,32,128]{2,1,0:T(8,128)(2,1)S(1)}, bf16[16,32,128]{2,1,0:T(8,128)(2,1)S(1)}, u32[]{:S(2)}, u32[]{:S(2)}) %collective-permute-start.1) | collective-permute-done | bytes 131104 | tf_op jit(solution)/shard_map/ppermute | solution.py:248
  31.2 0.0 all-to-all-done.parts_ref
  31.2 0.8 %owner_sum.1 = f32[32,16,128]{2,1,0:T(8,128)} custom-call(bf16[16,32,128]{2,1,0:T(8,128)(2,1)S(1)} %collective-permute-done.token_a_ref, bf16[16,32,128]{2,1,0:T(8,128)(2,1)S(1)} %collective-permute-done.1.token_b_ref, bf16[32,16,128]{2,1,0:T(8,128)(2,1)S(1)} %all-to-all-done.parts_ref), custom_call_target="tpu_custom_call" | custom-call | tf_op jit(solution)/shard_map/owner_sum/pallas_call | solution.py:251
  31.9 11.4 %all-to-all-start.1 = ((f32[32,16,128]{2,1,0:T(8,128)}), f32[32,16,128]{2,1,0:T(8,128)S(1)}, u32[]{:S(2)}, u32[]{:S(2)}) async-start(f32[32,16,128]{2,1,0:T(8,128)} %owner_sum.1), calls=%async_computation.1 | async-start | bytes 524288 | tf_op jit(solution)/shard_map/all_to_all | solution.py:260
  43.3 2.1 %collective-permute-start.2 = (bf16[32,32,128]{2,1,0:T(8,128)(2,1)S(1)}, bf16[32,32,128]{2,1,0:T(8,128)(2,1)S(1)}, u32[]{:S(2)}, u32[]{:S(2)}) collective-permute-start(bf16[32,32,128]{2,1,0:T(8,128)(2,1)S(1)} %get-tuple-element.10), channel_id=1, source_target_pairs={{32,0},{64,32},{96,64},{128,96},{160,128},{192,160},{224,192},{256... | collective-permute-start | bytes 786440 | tf_op jit(solution)/shard_map/ppermute | solution.py:249
  45.5 8.4 %all-to-all-done.1 = f32[32,16,128]{2,1,0:T(8,128)S(1)} async-done(((f32[32,16,128]{2,1,0:T(8,128)}), f32[32,16,128]{2,1,0:T(8,128)S(1)}, u32[]{:S(2)}, u32[]{:S(2)}) %all-to-all-start.1) | async-done | bytes 262176 | tf_op jit(solution)/shard_map/all_to_all | solution.py:260
  53.9 0.0 copy-start.2
  53.9 4.4 %all_gather.3.sums_ref = f32[2,512,128]{2,1,0:T(8,128)S(1)} all-gather(f32[1,512,128]{2,1,0:T(8,128)S(1)} %bitcast.15), channel_id=1, replica_groups=mesh['z'=8,'xl'=2,'y'=8,'xh'=2,'core'=2] {'core'}, dimensions={0}, use_global_device_ids=true | all-gather | bytes 786432 | tf_op jit(solution)/shard_map/all_gather | solution.py:261
  58.3 0.0 collective-permute-done.2.after_ref
  58.3 0.0 copy-done.2
  58.3 4.7 %advance.1 = bf16[32,64,128]{2,1,0:T(8,128)(2,1)} custom-call(s32[1]{0:T(128)} %bitcast.side_ref, s32[3,32]{1,0:T(4,128)S(1)} %copy-done.2, f32[2,512,128]{2,1,0:T(8,128)S(1)} %all_gather.3.sums_ref, bf16[32,32,128]{2,1,0:T(8,128)(2,1)S(1)} %pad_maximum_fusion.before_ref, bf16[32,64,128]{2,1,0:T(8,128)(2,1)S(1)} %bitcast.14, ...), custom_call_target="tpu_custom_call" | custom-call | tf_op jit(solution)/shard_map/advance/pallas_call | solution.py:262
  (1 shorter events, 0.0 us)
Async XLA Ops:
  0.0 13.6 %copy-start = (bf16[32,2,4096]{2,1,0:T(2,128)(2,1)S(1)}, bf16[32,2,4096]{2,1,0:T(2,128)(2,1)}, u32[]{:S(2)}) copy-start(bf16[32,2,4096]{2,1,0:T(2,128)(2,1)} %param.3) | copy-start | bytes 1572868
  2.2 11.4 %copy-start.1 = (bf16[32,16,128]{2,1,0:T(8,128)(2,1)S(1)}, bf16[32,16,128]{2,1,0:T(8,128)(2,1)}, u32[]{:S(2)}) copy-start(bf16[32,16,128]{2,1,0:T(8,128)(2,1)} %moments.1.token_ref) | copy-start | bytes 393220
  2.3 28.9 %all-to-all-start = ((bf16[32,16,128]{2,1,0:T(8,128)(2,1)}), bf16[32,16,128]{2,1,0:T(8,128)(2,1)S(1)}, u32[]{:S(2)}, u32[]{:S(2)}) async-start(bf16[32,16,128]{2,1,0:T(8,128)(2,1)} %moments.1.token_ref), calls=%async_computation | async-start | bytes 262144 | tf_op jit(solution)/shard_map/all_to_all | solution.py:230
  13.9 14.4 %collective-permute-start = (bf16[16,32,128]{2,1,0:T(8,128)(2,1)S(1)}, bf16[16,32,128]{2,1,0:T(8,128)(2,1)S(1)}, u32[]{:S(2)}, u32[]{:S(2)}) collective-permute-start(bf16[16,32,128]{2,1,0:T(8,128)(2,1)S(1)} %get-tuple-element.8), channel_id=1, source_target_pairs={{0,32},{32,64},{64,96},{96,128},{128,160},{160,192},{192,224},{224... | collective-permute-start | bytes 393224 | tf_op jit(solution)/shard_map/ppermute | solution.py:247
  16.2 15.0 %collective-permute-start.1 = (bf16[16,32,128]{2,1,0:T(8,128)(2,1)S(1)}, bf16[16,32,128]{2,1,0:T(8,128)(2,1)S(1)}, u32[]{:S(2)}, u32[]{:S(2)}) collective-permute-start(bf16[16,32,128]{2,1,0:T(8,128)(2,1)S(1)} %get-tuple-element.9), channel_id=1, source_target_pairs={{0,32},{32,64},{64,96},{96,128},{128,160},{160,192},{192,224},{224... | collective-permute-start | bytes 393224 | tf_op jit(solution)/shard_map/ppermute | solution.py:248
  31.9 22.0 %all-to-all-start.1 = ((f32[32,16,128]{2,1,0:T(8,128)}), f32[32,16,128]{2,1,0:T(8,128)S(1)}, u32[]{:S(2)}, u32[]{:S(2)}) async-start(f32[32,16,128]{2,1,0:T(8,128)} %owner_sum.1), calls=%async_computation.1 | async-start | bytes 524288 | tf_op jit(solution)/shard_map/all_to_all | solution.py:260
  43.3 15.0 %collective-permute-start.2 = (bf16[32,32,128]{2,1,0:T(8,128)(2,1)S(1)}, bf16[32,32,128]{2,1,0:T(8,128)(2,1)S(1)}, u32[]{:S(2)}, u32[]{:S(2)}) collective-permute-start(bf16[32,32,128]{2,1,0:T(8,128)(2,1)S(1)} %get-tuple-element.10), channel_id=1, source_target_pairs={{32,0},{64,32},{96,64},{128,96},{160,128},{192,160},{224,192},{256... | collective-permute-start | bytes 786440 | tf_op jit(solution)/shard_map/ppermute | solution.py:249
  53.9 4.4 %copy-start.2 = (s32[3,32]{1,0:T(4,128)S(1)}, s32[3,32]{1,0:T(4,128)}, u32[]{:S(2)}) copy-start(s32[3,32]{1,0:T(4,128)} %index_ref.1) | copy-start | bytes 1156

commit v4 on v2

v4 whole, which is shorter than its diff:
```python
import jax
import jax.numpy as jnp
import numpy as np
from jax import lax
from jax.experimental import pallas as pl
from jax.experimental.pallas import tpu as pltpu
from jax.sharding import Mesh, PartitionSpec as P

NV = 1024
NODES = 33
ROWS = 32
LANES = 128
CELLS = (ROWS, LANES)
BOTH = (2 * ROWS, LANES)

speed_max = 4.0
time_step = 1.0 / 12.0
relax_coef = 0.1
center = 24.0
log2e = 1.4426950408889634

SIZES = (8, 2, 8, 2, 2)
NAMES = ("z", "xl", "y", "xh", "core")
GX = ("z", "xl")
VERT = ("y", "xh", "core")

VMEM = pl.BlockSpec(memory_space=pltpu.VMEM)
HBM = pl.BlockSpec(memory_space=pltpu.HBM)
SMEM = pl.BlockSpec(memory_space=pltpu.SMEM)


HALF = ROWS // 2


def place(z, xl, y, xh, core):
    return ((((z % SIZES[0]) * 2 + xl) * SIZES[2] + y) * 2 + xh) * 2 + core


PAIRS = [[(z, 0, 0), (z, 1, 0)] for z in range(SIZES[0])] + [
    [(z, 1, 1), (z + 1, 0, 1)] for z in range(SIZES[0])
]
GROUPS = [
    [place(z, xl, y + odd, xh, core) for z, xl, core in pair for odd in range(2) for xh in range(2)]
    for pair in PAIRS
    for y in range(0, SIZES[2], 2)
]
NODE_SPEEDS = [float(speed_max * np.cos(np.pi * j / (NODES - 1))) for j in range(NODES)]


def fill_nodes(node_ref):
    for j, speed in enumerate(NODE_SPEEDS):
        node_ref[j] = jnp.float32(speed)


def small(mebibytes):
    return pltpu.CompilerParams(vmem_limit_bytes=mebibytes << 20)


def moments_kernel(
    index_hbm, weight_hbm, dist_hbm, out_ref,
    index_ref, weight_ref, node_ref, factor_ref, dist_ref, sums_ref, table_sems, sems,
):
    count = dist_ref.shape[0]
    half = count // 2
    pieces = []
    for part in range(2):
        for k in range(2):
            where = (pl.ds(k * half, half), pl.ds(part * ROWS, ROWS))
            pieces.append(pltpu.make_async_copy(dist_hbm.at[where], dist_ref.at[where], sems.at[2 * part + k]))
    tables = [
        pltpu.make_async_copy(index_hbm, index_ref, table_sems.at[0]),
        pltpu.make_async_copy(weight_hbm, weight_ref, table_sems.at[1]),
    ]
    for copy in tables + pieces:
        copy.start()
    fill_nodes(node_ref)
    for copy in tables:
        copy.wait()
    for v in range(count):
        sx = node_ref[index_ref[0, v]]
        sy = node_ref[index_ref[1, v]]
        sz = node_ref[index_ref[2, v]]
        weight = weight_ref[v].astype(jnp.float32) * (512.0 / (32768.0 * NV))
        factor_ref[0, v] = weight
        factor_ref[1, v] = weight * sx
        factor_ref[2, v] = weight * sy
        factor_ref[3, v] = weight * sz
        factor_ref[4, v] = weight * (sx * sx + sy * sy + sz * sz - center)
    for part in range(2):
        rows = pl.ds(part * ROWS, ROWS)
        sums = [jnp.zeros(CELLS, jnp.float32) for _ in range(5)]
        for v in range(count):
            if v % half == 0:
                pieces[2 * part + v // half].wait()
            value = dist_ref[v, rows, :].astype(jnp.float32)
            sums = [total + factor_ref[comp, v] * value for comp, total in enumerate(sums)]
        for comp in range(5):
            sums_ref[comp, rows, :] = sums[comp]
    for plane in range(2):
        for comp in range(5):
            out_ref[plane, comp] = sums_ref[comp, pl.ds(plane, ROWS, stride=2), :]


def chip_kernel(plane_ref, both_ref, out_ref):
    plane = plane_ref[0]
    for comp in range(5):
        total = (both_ref[0, plane, comp] + both_ref[1, plane, comp]).astype(out_ref.dtype)
        for y in range(out_ref.shape[0]):
            first = HALF * (y % 2)
            out_ref[y, comp] = total[first:first + HALF]


def split_kernel(side_ref, dist_ref, within_ref, passed_ref, rows_ref):
    side = side_ref[0]

    def step(v, carry):
        slot = v & 3
        rows_ref[slot] = dist_ref[v].astype(jnp.float32)
        within_ref[v] = rows_ref[slot, pl.ds(side, ROWS, stride=2), :].astype(jnp.bfloat16)
        passed_ref[v] = rows_ref[slot, pl.ds(1 - side, ROWS, stride=2), :].astype(jnp.bfloat16)
        return carry

    lax.fori_loop(0, dist_ref.shape[0], step, 0, unroll=4)


def column_kernel(parts_ref, out_ref):
    for comp in range(5):
        total = parts_ref[0, comp].astype(jnp.float32)
        for part in range(1, parts_ref.shape[0]):
            total = total + parts_ref[part, comp].astype(jnp.float32)
        for copy in range(out_ref.shape[0]):
            out_ref[copy, comp] = total


def advance_kernel(
    side_ref, index_ref, sums_ref, across_ref, dist_ref, within_ref, out_ref,
    node_ref, own_ref, edge_params_ref, edge_ref,
):
    side = side_ref[0]
    fill_nodes(node_ref)
    for plane, part in [(plane, part) for plane in range(4) for part in range(2)]:
        core, first = plane // 2, 4 * (plane % 2) + 2 * part
        core = core + (1 - side) * (1 - 2 * core)
        total = [sums_ref[core, first, comp] + sums_ref[core, first + 1, comp] for comp in range(5)]
        density = total[0]
        inverse = 1.0 / density
        flow = [total[comp] * inverse for comp in (1, 2, 3)]
        speed2 = flow[0] * flow[0] + flow[1] * flow[1] + flow[2] * flow[2]
        temper = (total[4] * inverse + center - speed2) * (1.0 / 3.0)
        root = jnp.sqrt(temper)
        rate = (time_step * relax_coef) * density * root
        scale = density * ((2.0 * np.pi) ** -1.5) / (temper * root)
        keep = 1.0 / (1.0 + rate)
        values = flow + [(-0.5 * log2e) / temper, scale * (rate * keep), keep]
        for comp in range(6):
            if plane in (1, 2):
                own_ref[comp, pl.ds(2 * HALF * part + plane - 1, HALF, stride=2), :] = values[comp]
            else:
                edge_params_ref[plane // 3, comp, pl.ds(HALF * part, HALF), :] = values[comp]
    lane8 = lax.broadcasted_iota(jnp.int32, (8,128), 1)
    sub8 = lax.broadcasted_iota(jnp.int32, (8,128), 0)
    column = lane8 & 63; upper = lane8 >> 6; parity = sub8 & 1

    def relax(value, params, sx, sy, sz):
        dx = sx - params(0); dy = sy - params(1); dz = sz - params(2)
        spread = dx * dx + dy * dy + dz * dz
        equil = params(4) * jnp.exp2(spread * params(3))
        return (value.astype(jnp.float32) * params(5) + equil).astype(jnp.bfloat16).astype(jnp.float32)

    def step(v, carry):
        sx = node_ref[index_ref[0, v]]
        sy = node_ref[index_ref[1, v]]
        sz = node_ref[index_ref[2, v]]
        up_x, up_y, up_z = sx > 0.0, sy > 0.0, sz > 0.0
        ax, ay, az = (time_step * jnp.abs(s) for s in (sx, sy, sz))
        rest = 1.0 - (ax + ay + az)
        which = jnp.where(up_x, 0, 1)
        edge_value = jnp.where(which == side, across_ref[v].astype(jnp.float32), within_ref[v].astype(jnp.float32))
        edge = relax(edge_value, lambda c: edge_params_ref[which, c], sx, sy, sz)
        slot = lax.rem(v, edge_ref.shape[0])
        edge_ref[slot, pl.ds(0, ROWS, stride=2), :] = edge
        edge_ref[slot, pl.ds(1, ROWS, stride=2), :] = edge
        xmask = parity == which
        s1 = jnp.where(up_x, 1, 7); s2 = jnp.where(up_y, 2, 6)
        xlast = sub8 == jnp.where(up_x, 0, 7)
        ylast = (sub8 >> 1) == jnp.where(up_y, 0, 3)
        ymask = upper == jnp.where(up_y, 0, 1)
        zmask = column == jnp.where(up_z, 0, 63)
        shift_z = jnp.where(up_z, 1, LANES - 1)
        raw = dist_ref[v].astype(jnp.float32)
        vals=[relax(raw[8*k:8*k+8], lambda c, k=k: own_ref[c, 8*k:8*k+8, :], sx, sy, sz) for k in range(8)]
        sw=[pltpu.roll(a,64,1) for a in vals]
        ry=[pltpu.roll(a,s2,0) for a in sw]
        rx=[pltpu.roll(a,s1,0) for a in vals]
        outs=[]
        for k in range(8):
            e = edge_ref[slot, 8*k:8*k+8, :]
            from_x = jnp.where(xmask, e, rx[k])
            nb = jnp.where(up_y, ry[(k-1)%8], ry[(k+1)%8])
            row = jnp.where(ylast, nb, ry[k])
            from_y = jnp.where(ymask, row, sw[k])
            near = pltpu.roll(vals[k], shift_z, 1)
            from_z = jnp.where(zmask, pltpu.roll(near, 64, 1), near)
            outs.append(rest*vals[k]+ax*from_x+ay*from_y+az*from_z)
        out_ref[v] = jnp.concatenate(outs,0).astype(jnp.bfloat16)
        return carry
    lax.fori_loop(0, dist_ref.shape[0], step, 0, unroll=8)


def shards(dist, vel_index, weight_int):
    count_v = dist.shape[0]
    side = lax.axis_index("xl")
    core = lax.axis_index("core")
    plane = jnp.reshape(1 ^ side ^ core, (1,)).astype(jnp.int32)
    side = jnp.reshape(side, (1,)).astype(jnp.int32)
    f32, bf16 = jnp.float32, jnp.bfloat16
    mixed = dist.reshape(count_v, 2, ROWS, LANES).transpose(0, 2, 1, 3).reshape((count_v,) + BOTH)

    partial_sums = pl.pallas_call(
        moments_kernel,
        out_shape=jax.ShapeDtypeStruct((2, 5) + CELLS, f32),
        in_specs=[HBM, HBM, HBM],
        out_specs=VMEM,
        scratch_shapes=[
            pltpu.SMEM(vel_index.shape, jnp.int32),
            pltpu.SMEM(weight_int.shape, jnp.int32),
            pltpu.SMEM((NODES,), f32),
            pltpu.SMEM((5, count_v), f32),
            pltpu.VMEM(mixed.shape, bf16),
            pltpu.VMEM((5,) + BOTH, f32),
            pltpu.SemaphoreType.DMA((2,)),
            pltpu.SemaphoreType.DMA((4,)),
        ],
        compiler_params=small(56),
        name="moments",
    )(vel_index, weight_int, mixed)
    both = lax.all_gather(partial_sums, "core")
    chip = pl.pallas_call(
        chip_kernel,
        out_shape=jax.ShapeDtypeStruct((SIZES[2], 5, HALF, LANES), bf16),
        in_specs=[SMEM, VMEM],
        out_specs=VMEM,
        compiler_params=small(4),
        name="chip_sum",
    )(plane, both)
    parts = lax.all_to_all(chip, "y", 0, 0)

    count = SIZES[0] * SIZES[1]
    beside = lax.ppermute(mixed, GX, [(i, i ^ 1) for i in range(count)])
    half = jax.ShapeDtypeStruct((count_v,) + CELLS, bf16)
    within, passed = pl.pallas_call(
        split_kernel,
        out_shape=(half, half),
        in_specs=[SMEM, VMEM],
        out_specs=(VMEM, VMEM),
        scratch_shapes=[pltpu.VMEM((4,) + BOTH, f32)],
        compiler_params=small(8),
        cost_estimate=pl.CostEstimate(flops=1 << 20, bytes_accessed=1 << 20, transcendentals=0),
        name="split_planes",
    )(side, beside)
    across = lax.ppermute(passed, GX, [(i, (i + 2 - 4 * (i % 2)) % count) for i in range(count)])

    column = pl.pallas_call(
        column_kernel,
        out_shape=jax.ShapeDtypeStruct((8, 5, HALF, LANES), f32),
        in_specs=[VMEM],
        out_specs=VMEM,
        compiler_params=small(4),
        name="column_sum",
    )(parts)
    gathered = lax.all_to_all(column, NAMES, 0, 0, axis_index_groups=GROUPS)
    sums = lax.all_gather(gathered, "core")
    out = pl.pallas_call(
        advance_kernel,
        out_shape=jax.ShapeDtypeStruct(mixed.shape, bf16),
        in_specs=[SMEM, SMEM, VMEM, VMEM, VMEM, VMEM],
        out_specs=VMEM,
        scratch_shapes=[
            pltpu.SMEM((NODES,), f32),
            pltpu.VMEM((6,) + BOTH, f32),
            pltpu.VMEM((2, 6) + CELLS, f32),
            pltpu.VMEM((8,) + BOTH, f32),
        ],
        compiler_params=small(16),
        name="advance",
    )(side, vel_index, sums, across, mixed, within)
    return out.reshape(count_v, ROWS, 2, LANES).transpose(0, 2, 1, 3).reshape(dist.shape)


def solution(mesh):
    parts = Mesh(mesh.devices.reshape(SIZES), NAMES)
    return jax.shard_map(
        shards,
        mesh=parts,
        in_specs=(P(VERT, GX, None), P(None, VERT), P(VERT)),
        out_specs=P(VERT, GX, None),
        check_vma=False,
    )
```

time: 53.9 us -> 49.7 us (0.922)
  blocking collectives: 24.7 us -> 11 us
  waiting for transfers between devices: 5.33 us -> 13 us
  starting transfers between devices: 14.9 us -> 17.9 us
  local copies, waits for them, and re-layouts: 1.73 us -> 0.01 us
    all_to_all x1 -> x0, blocking collectives: 13.9 us -> none  [shards(): quad = lax.all_to_all(column, QUAD, 0, 0, axis_index_groups=QUADS)]
    all_to_all x0 -> x1, starting transfers between devices: none -> 10.7 us  [shards(): gathered = lax.all_to_all(column, NAMES, 0, 0, axis_index_groups=GROUPS)]
    ppermute x2, starting transfers between devices: 11.5 us -> 3.84 us  [the longest x1 1.92 us: shards(): beside = lax.ppermute(mixed, GX, [(i, i ^ 1) for i in range(count)])]
    all_to_all x1, waiting for transfers between devices: 0.01 us -> 7.11 us  [shards(): parts = lax.all_to_all(chip, 'y', 0, 0)]
    all_to_all x0 -> x1, waiting for transfers between devices: none -> 3.97 us  [shards(): gathered = lax.all_to_all(column, NAMES, 0, 0, axis_index_groups=GROUPS)]
    ppermute x2, waiting for transfers between devices: 5.33 us -> 1.94 us  [the longest x1 1.94 us: shards(): lax.ppermute(passed, GX, [(i, (i + 2 - 4 * (i % 2)) % count) for i in ran...]
    unnamed x10 -> x4, local copies, waits for them, and re-layouts: 1.73 us -> 0.01 us
    pallas_call x1, Pallas kernels: 4.57 us -> 3.15 us  [shards(): pl.pallas_call(advance_kernel, out_shape=jax.ShapeDtypeStruct(mixed.shape...]
  transfers between devices with their start and end apart: 3 -> 4, of which waited for: 2 -> 3; matrix products, arithmetic and copies ran while one was open for 0% -> 0% of each run, Pallas kernels for 1% -> 2%
where the time goes in v4:
time: 49.7 us; the launch traced here: 49 us
  starting transfers between devices  17.9 us (36%)
  waiting for transfers between devices  13 us (26%)
  blocking collectives  11 us (22%)
  Pallas kernels  7.03 us (14%)
    all_to_all x1, starting transfers between devices, shards(): gathered = lax.all_to_all(column, NAMES, 0, 0, axis_index_groups=GROUPS)  10.7 us
    all_gather x1, blocking collectives, shards(): both = lax.all_gather(partial_sums, 'core')  8.76 us
    all_to_all x1, waiting for transfers between devices, shards(): parts = lax.all_to_all(chip, 'y', 0, 0)  7.11 us
    all_to_all x1, waiting for transfers between devices, shards(): gathered = lax.all_to_all(column, NAMES, 0, 0, axis_index_groups=GROUPS)  3.97 us
    all_to_all x1, starting transfers between devices, shards(): parts = lax.all_to_all(chip, 'y', 0, 0)  3.38 us
    pallas_call x1, Pallas kernels, shards(): pl.pallas_call(advance_kernel, out_shape=jax.ShapeDtypeStruct(mixed.shape...  3.15 us
    all_gather x1, blocking collectives, shards(): sums = lax.all_gather(gathered, 'core')  2.26 us
    pallas_call x1, Pallas kernels, shards(): pl.pallas_call(moments_kernel, out_shape=jax.ShapeDtypeStruct((2, 5) + CE...  2.15 us
  transfers between devices with their start and end apart: 4, of which 3 were waited for; matrix products, arithmetic and copies ran while one was open for 0% of the time, Pallas kernels for 2%

profile of v4, /device:TPU:1, one launch (start us, length us, event | category | flops | bytes accessed | tf_op | source)
XLA Modules:
  0.0 49.0 jit_solution(1327205618346861521)
XLA Ops:
  0.0 2.1 %moments.1 = f32[2,5,32,128]{3,2,1,0:T(8,128)} custom-call(s32[3,32]{1,0:T(4,128)} %index_ref.1, s32[32]{0:T(128)} %weight_hbm.1, bf16[32,64,128]{2,1,0:T(8,128)(2,1)} %bitcast.15), custom_call_target="tpu_custom_call" | custom-call | tf_op jit(solution)/shard_map/moments/pallas_call | solution.py:219
  2.2 8.8 %all-gather = f32[4,5,32,128]{3,2,1,0:T(8,128)S(1)} all-gather(f32[2,5,32,128]{3,2,1,0:T(8,128)} %moments.1), channel_id=2, replica_groups=mesh['z'=8,'xl'=2,'y'=8,'xh'=2,'core'=2] {'core'}, dimensions={0}, use_global_device_ids=true | all-gather | bytes 491520 | tf_op jit(solution)/shard_map/all_gather | solution.py:237
  10.9 0.0 copy-start
  10.9 0.7 %chip_sum.1 = bf16[8,5,16,128]{3,2,1,0:T(8,128)(2,1)} custom-call(s32[1]{0:T(128)} %bitcast.1.plane_ref, f32[2,2,5,32,128]{4,3,2,1,0:T(8,128)S(1)} %bitcast.18), custom_call_target="tpu_custom_call" | custom-call | tf_op jit(solution)/shard_map/chip_sum/pallas_call | solution.py:238
  11.6 3.4 %all-to-all-start = ((bf16[8,5,16,128]{3,2,1,0:T(8,128)(2,1)}), bf16[8,5,16,128]{3,2,1,0:T(8,128)(2,1)S(1)}, u32[]{:S(2)}, u32[]{:S(2)}) async-start(bf16[8,5,16,128]{3,2,1,0:T(8,128)(2,1)} %chip_sum.1), calls=%async_computation | async-start | bytes 327680 | tf_op jit(solution)/shard_map/all_to_all | solution.py:246
  15.0 0.0 copy-done
  15.0 1.9 %collective-permute-start = (bf16[32,64,128]{2,1,0:T(8,128)(2,1)S(1)}, bf16[32,64,128]{2,1,0:T(8,128)(2,1)S(1)}, u32[]{:S(2)}, u32[]{:S(2)}) collective-permute-start(bf16[32,64,128]{2,1,0:T(8,128)(2,1)S(1)} %bitcast.16), channel_id=1, source_target_pairs={{0,32},{32,0},{64,96},{96,64},{128,160},{160,128},{192,224},{224,1... | collective-permute-start | bytes 1572872 | tf_op jit(solution)/shard_map/ppermute | solution.py:249
  16.9 7.1 %all-to-all-done.parts_ref = bf16[8,5,16,128]{3,2,1,0:T(8,128)(2,1)S(1)} async-done(((bf16[8,5,16,128]{3,2,1,0:T(8,128)(2,1)}), bf16[8,5,16,128]{3,2,1,0:T(8,128)(2,1)S(1)}, u32[]{:S(2)}, u32[]{:S(2)}) %all-to-all-start) | async-done | bytes 163872 | tf_op jit(solution)/shard_map/all_to_all | solution.py:246
  24.0 0.8 %column_sum.1 = f32[8,5,16,128]{3,2,1,0:T(8,128)} custom-call(bf16[8,5,16,128]{3,2,1,0:T(8,128)(2,1)S(1)} %all-to-all-done.parts_ref), custom_call_target="tpu_custom_call" | custom-call | tf_op jit(solution)/shard_map/column_sum/pallas_call | solution.py:263
  24.8 10.7 %all-to-all-start.1 = ((f32[8,5,16,128]{3,2,1,0:T(8,128)}), f32[8,5,16,128]{3,2,1,0:T(8,128)S(1)}, u32[]{:S(2)}, u32[]{:S(2)}) async-start(f32[8,5,16,128]{3,2,1,0:T(8,128)} %column_sum.1), calls=%async_computation.1 | async-start | bytes 655360 | tf_op jit(solution)/shard_map/all_to_all | solution.py:271
  35.5 0.0 collective-permute-done.dist_ref
  35.5 0.3 split_planes.1
  35.8 1.9 %collective-permute-start.1 = (bf16[32,32,128]{2,1,0:T(8,128)(2,1)S(1)}, bf16[32,32,128]{2,1,0:T(8,128)(2,1)S(1)}, u32[]{:S(2)}, u32[]{:S(2)}) collective-permute-start(bf16[32,32,128]{2,1,0:T(8,128)(2,1)S(1)} %get-tuple-element.7), channel_id=1, source_target_pairs={{0,64},{32,480},{64,128},{96,32},{128,192},{160,96},{192,256},{224... | collective-permute-start | bytes 786440 | tf_op jit(solution)/shard_map/ppermute | solution.py:261
  37.7 4.0 %all-to-all-done.1 = f32[8,5,16,128]{3,2,1,0:T(8,128)S(1)} async-done(((f32[8,5,16,128]{3,2,1,0:T(8,128)}), f32[8,5,16,128]{3,2,1,0:T(8,128)S(1)}, u32[]{:S(2)}, u32[]{:S(2)}) %all-to-all-start.1) | async-done | bytes 327712 | tf_op jit(solution)/shard_map/all_to_all | solution.py:271
  41.7 2.3 %all-gather.1 = f32[16,5,16,128]{3,2,1,0:T(8,128)S(1)} all-gather(f32[8,5,16,128]{3,2,1,0:T(8,128)S(1)} %all-to-all-done.1), channel_id=3, replica_groups=mesh['z'=8,'xl'=2,'y'=8,'xh'=2,'core'=2] {'core'}, dimensions={0}, use_global_device_ids=true | all-gather | bytes 983040 | tf_op jit(solution)/shard_map/all_gather | solution.py:272
  43.9 0.0 copy-start.1
  43.9 1.9 %collective-permute-done.1.across_ref = bf16[32,32,128]{2,1,0:T(8,128)(2,1)S(1)} collective-permute-done((bf16[32,32,128]{2,1,0:T(8,128)(2,1)S(1)}, bf16[32,32,128]{2,1,0:T(8,128)(2,1)S(1)}, u32[]{:S(2)}, u32[]{:S(2)}) %collective-permute-start.1) | collective-permute-done | bytes 262176 | tf_op jit(solution)/shard_map/ppermute | solution.py:261
  45.9 0.0 copy-done.1
  45.9 3.1 %advance.1 = bf16[32,64,128]{2,1,0:T(8,128)(2,1)} custom-call(s32[1]{0:T(128)} %bitcast.side_ref, s32[3,32]{1,0:T(4,128)S(1)} %copy-done.1, f32[2,8,5,16,128]{4,3,2,1,0:T(8,128)S(1)} %bitcast.14, bf16[32,32,128]{2,1,0:T(8,128)(2,1)S(1)} %collective-permute-done.1.across_ref, bf16[32,64,128]{2,1,0:T(8,128)(2,1)S(1)} %bitcast.17, ...), custom_call_target="tpu_custom_call" | custom-call | tf_op jit(solution)/shard_map/advance/pallas_call | solution.py:273
Async XLA Ops:
  10.9 4.1 %copy-start = (bf16[32,2,4096]{2,1,0:T(2,128)(2,1)S(1)}, bf16[32,2,4096]{2,1,0:T(2,128)(2,1)}, u32[]{:S(2)}) copy-start(bf16[32,2,4096]{2,1,0:T(2,128)(2,1)} %param.3) | copy-start | bytes 1572868
  11.6 12.4 %all-to-all-start = ((bf16[8,5,16,128]{3,2,1,0:T(8,128)(2,1)}), bf16[8,5,16,128]{3,2,1,0:T(8,128)(2,1)S(1)}, u32[]{:S(2)}, u32[]{:S(2)}) async-start(bf16[8,5,16,128]{3,2,1,0:T(8,128)(2,1)} %chip_sum.1), calls=%async_computation | async-start | bytes 327680 | tf_op jit(solution)/shard_map/all_to_all | solution.py:246
  15.0 20.5 %collective-permute-start = (bf16[32,64,128]{2,1,0:T(8,128)(2,1)S(1)}, bf16[32,64,128]{2,1,0:T(8,128)(2,1)S(1)}, u32[]{:S(2)}, u32[]{:S(2)}) collective-permute-start(bf16[32,64,128]{2,1,0:T(8,128)(2,1)S(1)} %bitcast.16), channel_id=1, source_target_pairs={{0,32},{32,0},{64,96},{96,64},{128,160},{160,128},{192,224},{224,1... | collective-permute-start | bytes 1572872 | tf_op jit(solution)/shard_map/ppermute | solution.py:249
  24.8 16.9 %all-to-all-start.1 = ((f32[8,5,16,128]{3,2,1,0:T(8,128)}), f32[8,5,16,128]{3,2,1,0:T(8,128)S(1)}, u32[]{:S(2)}, u32[]{:S(2)}) async-start(f32[8,5,16,128]{3,2,1,0:T(8,128)} %column_sum.1), calls=%async_computation.1 | async-start | bytes 655360 | tf_op jit(solution)/shard_map/all_to_all | solution.py:271
  35.8 10.1 %collective-permute-start.1 = (bf16[32,32,128]{2,1,0:T(8,128)(2,1)S(1)}, bf16[32,32,128]{2,1,0:T(8,128)(2,1)S(1)}, u32[]{:S(2)}, u32[]{:S(2)}) collective-permute-start(bf16[32,32,128]{2,1,0:T(8,128)(2,1)S(1)} %get-tuple-element.7), channel_id=1, source_target_pairs={{0,64},{32,480},{64,128},{96,32},{128,192},{160,96},{192,256},{224... | collective-permute-start | bytes 786440 | tf_op jit(solution)/shard_map/ppermute | solution.py:261
  43.9 1.9 %copy-start.1 = (s32[3,32]{1,0:T(4,128)S(1)}, s32[3,32]{1,0:T(4,128)}, u32[]{:S(2)}) copy-start(s32[3,32]{1,0:T(4,128)} %index_ref.1) | copy-start | bytes 1156

commit v5 on v4

--- a/solution.py
+++ b/solution.py
@@ -52,13 +52,17 @@
         node_ref[j] = jnp.float32(speed)
 
 
+def scalars(index_ref, node_ref, v):
+    return [node_ref[index_ref[comp, v]] for comp in range(3)]
+
+
 def small(mebibytes):
     return pltpu.CompilerParams(vmem_limit_bytes=mebibytes << 20)
 
 
 def moments_kernel(
     index_hbm, weight_hbm, dist_hbm, out_ref,
-    index_ref, weight_ref, node_ref, factor_ref, dist_ref, sums_ref, table_sems, sems,
+    index_ref, weight_ref, node_ref, dist_ref, sums_ref, table_sems, sems,
 ):
     count = dist_ref.shape[0]
     half = count // 2
@@ -76,24 +80,18 @@
     fill_nodes(node_ref)
     for copy in tables:
         copy.wait()
-    for v in range(count):
-        sx = node_ref[index_ref[0, v]]
-        sy = node_ref[index_ref[1, v]]
-        sz = node_ref[index_ref[2, v]]
-        weight = weight_ref[v].astype(jnp.float32) * (512.0 / (32768.0 * NV))
-        factor_ref[0, v] = weight
-        factor_ref[1, v] = weight * sx
-        factor_ref[2, v] = weight * sy
-        factor_ref[3, v] = weight * sz
-        factor_ref[4, v] = weight * (sx * sx + sy * sy + sz * sz - center)
     for part in range(2):
         rows = pl.ds(part * ROWS, ROWS)
         sums = [jnp.zeros(CELLS, jnp.float32) for _ in range(5)]
         for v in range(count):
             if v % half == 0:
                 pieces[2 * part + v // half].wait()
-            value = dist_ref[v, rows, :].astype(jnp.float32)
-            sums = [total + factor_ref[comp, v] * value for comp, total in enumerate(sums)]
+            sx, sy, sz = scalars(index_ref, node_ref, v)
+            weight = weight_ref[v].astype(jnp.float32) * (512.0 / (32768.0 * NV))
+            square = sx * sx + sy * sy + sz * sz - center
+            value = weight * dist_ref[v, rows, :].astype(jnp.float32)
+            terms = (value, sx * value, sy * value, sz * value, square * value)
+            sums = [total + term for total, term in zip(sums, terms)]
         for comp in range(5):
             sums_ref[comp, rows, :] = sums[comp]
     for plane in range(2):
@@ -110,14 +108,18 @@
             out_ref[y, comp] = total[first:first + HALF]
 
 
-def split_kernel(side_ref, dist_ref, within_ref, passed_ref, rows_ref):
+def copy_kernel(in_ref, out_ref):
+    out_ref[...] = in_ref[...]
+
+
+def split_kernel(side_ref, dist_ref, far_ref, near_ref, rows_ref):
     side = side_ref[0]
 
     def step(v, carry):
         slot = v & 3
         rows_ref[slot] = dist_ref[v].astype(jnp.float32)
-        within_ref[v] = rows_ref[slot, pl.ds(side, ROWS, stride=2), :].astype(jnp.bfloat16)
-        passed_ref[v] = rows_ref[slot, pl.ds(1 - side, ROWS, stride=2), :].astype(jnp.bfloat16)
+        far_ref[v] = rows_ref[slot, pl.ds(side, ROWS, stride=2), :].astype(jnp.bfloat16)
+        near_ref[v] = rows_ref[slot, pl.ds(1 - side, ROWS, stride=2), :].astype(jnp.bfloat16)
         return carry
 
     lax.fori_loop(0, dist_ref.shape[0], step, 0, unroll=4)
@@ -132,9 +134,20 @@
             out_ref[copy, comp] = total
 
 
-def advance_kernel(
-    side_ref, index_ref, sums_ref, across_ref, dist_ref, within_ref, out_ref,
-    node_ref, own_ref, edge_params_ref, edge_ref,
+def equilibrium(params, sx, sy, sz):
+    dx, dy, dz = sx - params(0), sy - params(1), sz - params(2)
+    spread = dx * dx + dy * dy + dz * dz
+    return params(4) * jnp.exp2(spread * params(3))
+
+
+def relax(value, params, sx, sy, sz):
+    mixed = value * params(5) + equilibrium(params, sx, sy, sz)
+    return mixed.astype(jnp.bfloat16).astype(jnp.float32)
+
+
+def inner_kernel(
+    side_ref, index_ref, sums_ref, dist_ref,
+    moved_ref, table_ref, equil_ref, edge_params_ref, node_ref, own_ref,
 ):
     side = side_ref[0]
     fill_nodes(node_ref)
@@ -157,54 +170,81 @@
                 own_ref[comp, pl.ds(2 * HALF * part + plane - 1, HALF, stride=2), :] = values[comp]
             else:
                 edge_params_ref[plane // 3, comp, pl.ds(HALF * part, HALF), :] = values[comp]
-    lane8 = lax.broadcasted_iota(jnp.int32, (8,128), 1)
-    sub8 = lax.broadcasted_iota(jnp.int32, (8,128), 0)
-    column = lane8 & 63; upper = lane8 >> 6; parity = sub8 & 1
-
-    def relax(value, params, sx, sy, sz):
-        dx = sx - params(0); dy = sy - params(1); dz = sz - params(2)
-        spread = dx * dx + dy * dy + dz * dz
-        equil = params(4) * jnp.exp2(spread * params(3))
-        return (value.astype(jnp.float32) * params(5) + equil).astype(jnp.bfloat16).astype(jnp.float32)
+
+    lane = lax.broadcasted_iota(jnp.int32, (8, LANES), 1)
+    row = lax.broadcasted_iota(jnp.int32, (8, LANES), 0)
+    column, upper, parity = lane & 63, lane >> 6, row & 1
+    blocks = 2 * ROWS // 8
 
     def step(v, carry):
-        sx = node_ref[index_ref[0, v]]
-        sy = node_ref[index_ref[1, v]]
-        sz = node_ref[index_ref[2, v]]
+        sx, sy, sz = scalars(index_ref, node_ref, v)
         up_x, up_y, up_z = sx > 0.0, sy > 0.0, sz > 0.0
         ax, ay, az = (time_step * jnp.abs(s) for s in (sx, sy, sz))
         rest = 1.0 - (ax + ay + az)
         which = jnp.where(up_x, 0, 1)
-        edge_value = jnp.where(which == side, across_ref[v].astype(jnp.float32), within_ref[v].astype(jnp.float32))
-        edge = relax(edge_value, lambda c: edge_params_ref[which, c], sx, sy, sz)
-        slot = lax.rem(v, edge_ref.shape[0])
+        halo_x = parity == which
+        table_ref[pl.ds(v, 1), :] = jnp.full((1, LANES), jnp.where(which == side, ax, -ax), jnp.float32)
+        equil_ref[v] = equilibrium(lambda c: edge_params_ref[which, c], sx, sy, sz)
+        shift_x = jnp.where(up_x, 1, 7)
+        shift_y = jnp.where(up_y, 2, 6)
+        last_y = (row >> 1) == jnp.where(up_y, 0, 3)
+        wrap_y = upper == jnp.where(up_y, 0, 1)
+        wrap_z = column == jnp.where(up_z, 0, 63)
+        shift_z = jnp.where(up_z, 1, LANES - 1)
+        values = []
+        for k in range(blocks):
+            rows = slice(8 * k, 8 * k + 8)
+            raw = dist_ref[v, 16 * (k // 2):16 * (k // 2) + 16, :].astype(jnp.float32)
+            part = raw[8 * (k % 2):8 * (k % 2) + 8]
+            values.append(relax(part, lambda c: own_ref[c, rows, :], sx, sy, sz))
+        swapped = [pltpu.roll(value, 64, 1) for value in values]
+        turned = [pltpu.roll(value, shift_y, 0) for value in swapped]
+        for k in range(blocks):
+            value = values[k]
+            from_x = jnp.where(halo_x, 0.0, pltpu.roll(value, shift_x, 0))
+            beyond = jnp.where(up_y, turned[(k - 1) % blocks], turned[(k + 1) % blocks])
+            from_y = jnp.where(wrap_y, jnp.where(last_y, beyond, turned[k]), swapped[k])
+            near = pltpu.roll(value, shift_z, 1)
+            from_z = jnp.where(wrap_z, pltpu.roll(near, 64, 1), near)
+            moved_ref[v, 8 * k:8 * k + 8, :] = rest * value + ax * from_x + ay * from_y + az * from_z
+        return carry
+
+    lax.fori_loop(0, dist_ref.shape[0], step, 0, unroll=8)
+
+
+def edge_kernel(
+    side_ref, table_ref, equil_ref, edge_params_ref, across_ref, within_ref, moved_ref, out_hbm,
+    out_ref, edge_ref, sems,
+):
+    side = side_ref[0]
+    keep_across = edge_params_ref[side, 5]
+    keep_within = edge_params_ref[1 - side, 5]
+    far_rows = (lax.broadcasted_iota(jnp.int32, BOTH, 0) & 1) == side
+    copies = sems.shape[0]
+    count = across_ref.shape[0] // copies
+
+    def step(v, slot):
+        size = table_ref[pl.ds(v, 1), :]
+        far = size > 0.0
+        value = jnp.where(far, across_ref[v].astype(jnp.float32), within_ref[v].astype(jnp.float32))
+        mixed = value * jnp.where(far, keep_across, keep_within) + equil_ref[v]
+        edge = mixed.astype(jnp.bfloat16).astype(jnp.float32) * jnp.abs(size)
         edge_ref[slot, pl.ds(0, ROWS, stride=2), :] = edge
         edge_ref[slot, pl.ds(1, ROWS, stride=2), :] = edge
-        xmask = parity == which
-        s1 = jnp.where(up_x, 1, 7); s2 = jnp.where(up_y, 2, 6)
-        xlast = sub8 == jnp.where(up_x, 0, 7)
-        ylast = (sub8 >> 1) == jnp.where(up_y, 0, 3)
-        ymask = upper == jnp.where(up_y, 0, 1)
-        zmask = column == jnp.where(up_z, 0, 63)
-        shift_z = jnp.where(up_z, 1, LANES - 1)
-        raw = dist_ref[v].astype(jnp.float32)
-        vals=[relax(raw[8*k:8*k+8], lambda c, k=k: own_ref[c, 8*k:8*k+8, :], sx, sy, sz) for k in range(8)]
-        sw=[pltpu.roll(a,64,1) for a in vals]
-        ry=[pltpu.roll(a,s2,0) for a in sw]
-        rx=[pltpu.roll(a,s1,0) for a in vals]
-        outs=[]
-        for k in range(8):
-            e = edge_ref[slot, 8*k:8*k+8, :]
-            from_x = jnp.where(xmask, e, rx[k])
-            nb = jnp.where(up_y, ry[(k-1)%8], ry[(k+1)%8])
-            row = jnp.where(ylast, nb, ry[k])
-            from_y = jnp.where(ymask, row, sw[k])
-            near = pltpu.roll(vals[k], shift_z, 1)
-            from_z = jnp.where(zmask, pltpu.roll(near, 64, 1), near)
-            outs.append(rest*vals[k]+ax*from_x+ay*from_y+az*from_z)
-        out_ref[v] = jnp.concatenate(outs,0).astype(jnp.bfloat16)
+        added = jnp.where(far == far_rows, edge_ref[slot], 0.0)
+        out_ref[v] = (moved_ref[v] + added).astype(jnp.bfloat16)
+
+    def chunk(c, carry):
+        for u in range(count):
+            step(c * count + u, u)
+        where = pl.ds(c * count, count)
+        pltpu.make_async_copy(out_ref.at[where], out_hbm.at[where], sems.at[c]).start()
         return carry
-    lax.fori_loop(0, dist_ref.shape[0], step, 0, unroll=8)
+
+    lax.fori_loop(0, copies, chunk, 0)
+    for c in range(copies):
+        where = pl.ds(c * count, count)
+        pltpu.make_async_copy(out_ref.at[where], out_hbm.at[where], sems.at[c]).wait()
 
 
 def shards(dist, vel_index, weight_int):
@@ -225,7 +265,6 @@
             pltpu.SMEM(vel_index.shape, jnp.int32),
             pltpu.SMEM(weight_int.shape, jnp.int32),
             pltpu.SMEM((NODES,), f32),
-            pltpu.SMEM((5, count_v), f32),
             pltpu.VMEM(mixed.shape, bf16),
             pltpu.VMEM((5,) + BOTH, f32),
             pltpu.SemaphoreType.DMA((2,)),
@@ -246,9 +285,10 @@
     parts = lax.all_to_all(chip, "y", 0, 0)
 
     count = SIZES[0] * SIZES[1]
-    beside = lax.ppermute(mixed, GX, [(i, i ^ 1) for i in range(count)])
+    swap = [(i, i ^ 1) for i in range(count)]
+    along = [(i, (i + 2 - 4 * (i % 2)) % count) for i in range(count)]
     half = jax.ShapeDtypeStruct((count_v,) + CELLS, bf16)
-    within, passed = pl.pallas_call(
+    far, near = pl.pallas_call(
         split_kernel,
         out_shape=(half, half),
         in_specs=[SMEM, VMEM],
@@ -257,8 +297,21 @@
         compiler_params=small(8),
         cost_estimate=pl.CostEstimate(flops=1 << 20, bytes_accessed=1 << 20, transcendentals=0),
         name="split_planes",
-    )(side, beside)
-    across = lax.ppermute(passed, GX, [(i, (i + 2 - 4 * (i % 2)) % count) for i in range(count)])
+    )(side, mixed)
+
+    def hand_on(planes, cost):
+        return pl.pallas_call(
+            copy_kernel,
+            out_shape=half,
+            in_specs=[VMEM],
+            out_specs=VMEM,
+            compiler_params=small(8),
+            cost_estimate=pl.CostEstimate(flops=cost, bytes_accessed=1 << 19, transcendentals=0),
+            name="hand_on",
+        )(planes)
+
+    across = lax.ppermute(hand_on(lax.ppermute(far, GX, swap), 1 << 31), GX, along)
+    within = hand_on(lax.ppermute(near, GX, swap), 1 << 32)
 
     column = pl.pallas_call(
         column_kernel,
@@ -270,20 +323,34 @@
     )(parts)
     gathered = lax.all_to_all(column, NAMES, 0, 0, axis_index_groups=GROUPS)
     sums = lax.all_gather(gathered, "core")
+    moved, table, equil, edge_params = pl.pallas_call(
+        inner_kernel,
+        out_shape=(
+            jax.ShapeDtypeStruct(mixed.shape, f32),
+            jax.ShapeDtypeStruct((count_v, LANES), f32),
+            jax.ShapeDtypeStruct((count_v,) + CELLS, f32),
+            jax.ShapeDtypeStruct((2, 6) + CELLS, f32),
+        ),
+        in_specs=[SMEM, SMEM, VMEM, VMEM],
+        out_specs=(VMEM, VMEM, VMEM, VMEM),
+        scratch_shapes=[pltpu.SMEM((NODES,), f32), pltpu.VMEM((6,) + BOTH, f32)],
+        compiler_params=small(8),
+        cost_estimate=pl.CostEstimate(flops=1, bytes_accessed=1, transcendentals=0),
+        name="inner",
+    )(side, vel_index, sums, mixed)
     out = pl.pallas_call(
-        advance_kernel,
+        edge_kernel,
         out_shape=jax.ShapeDtypeStruct(mixed.shape, bf16),
-        in_specs=[SMEM, SMEM, VMEM, VMEM, VMEM, VMEM],
-        out_specs=VMEM,
+        in_specs=[SMEM, VMEM, VMEM, VMEM, VMEM, VMEM, VMEM],
+        out_specs=HBM,
         scratch_shapes=[
-            pltpu.SMEM((NODES,), f32),
-            pltpu.VMEM((6,) + BOTH, f32),
-            pltpu.VMEM((2, 6) + CELLS, f32),
+            pltpu.VMEM(mixed.shape, bf16),
             pltpu.VMEM((8,) + BOTH, f32),
+            pltpu.SemaphoreType.DMA((4,)),
         ],
-        compiler_params=small(16),
-        name="advance",
-    )(side, vel_index, sums, across, mixed, within)
+        compiler_params=small(8),
+        name="edge",
+    )(side, table, equil, edge_params, across, within, moved)
     return out.reshape(count_v, ROWS, 2, LANES).transpose(0, 2, 1, 3).reshape(dist.shape)
 
 

time: 49.7 us -> 47.8 us (0.962)
  waiting for transfers between devices: 13 us -> 7.75 us
  starting transfers between devices: 17.9 us -> 21.2 us
    all_to_all x1, waiting for transfers between devices: 7.11 us -> 3.45 us  [shards(): parts = lax.all_to_all(chip, 'y', 0, 0)]
    ppermute x2 -> x3, starting transfers between devices: 3.84 us -> 7.2 us  [the longest x1 3.36 us: shards(): within = hand_on(lax.ppermute(near, GX, swap), 1 << 32)]
    ppermute x2 -> x3, waiting for transfers between devices: 1.94 us -> 0.1 us  [the longest x1 0.09 us: shards(): lax.ppermute(hand_on(lax.ppermute(far, GX, swap), 1 << 31), GX, along)]
    pallas_call x1 -> x4, Pallas kernels: 3.15 us -> 3.29 us  [the longest x1 2.15 us: shards(): pl.pallas_call(inner_kernel, out_shape=(jax.ShapeDtypeStruct(mixed.shape,...]
  transfers between devices with their start and end apart: 4 -> 5, of which waited for: 3 -> 3; matrix products, arithmetic and copies ran while one was open for 0% -> 0% of each run, Pallas kernels for 2% -> 7%
where the time goes in v5:
time: 47.8 us; the launch traced here: 47.3 us
  starting transfers between devices  21.2 us (44%)
  blocking collectives  11.2 us (23%)
  waiting for transfers between devices  7.75 us (16%)
  Pallas kernels  7.09 us (15%)
    all_to_all x1, starting transfers between devices, shards(): gathered = lax.all_to_all(column, NAMES, 0, 0, axis_index_groups=GROUPS)  10.7 us
    all_gather x1, blocking collectives, shards(): both = lax.all_gather(partial_sums, 'core')  8.76 us
    all_to_all x1, waiting for transfers between devices, shards(): gathered = lax.all_to_all(column, NAMES, 0, 0, axis_index_groups=GROUPS)  4.21 us
    all_to_all x1, waiting for transfers between devices, shards(): parts = lax.all_to_all(chip, 'y', 0, 0)  3.45 us
    all_to_all x1, starting transfers between devices, shards(): parts = lax.all_to_all(chip, 'y', 0, 0)  3.38 us
    ppermute x1, starting transfers between devices, shards(): within = hand_on(lax.ppermute(near, GX, swap), 1 << 32)  3.36 us
    all_gather x1, blocking collectives, shards(): sums = lax.all_gather(gathered, 'core')  2.39 us
    pallas_call x1, Pallas kernels, shards(): pl.pallas_call(inner_kernel, out_shape=(jax.ShapeDtypeStruct(mixed.shape,...  2.15 us
  transfers between devices with their start and end apart: 5, of which 3 were waited for; matrix products, arithmetic and copies ran while one was open for 0% of the time, Pallas kernels for 7%

profile of v5, /device:TPU:1, one launch (start us, length us, event | category | flops | bytes accessed | tf_op | source)
XLA Modules:
  0.0 47.3 jit_solution(386486848207080289)
XLA Ops:
  0.0 2.1 %moments.1 = f32[2,5,32,128]{3,2,1,0:T(8,128)} custom-call(s32[3,32]{1,0:T(4,128)} %index_ref.1, s32[32]{0:T(128)} %weight_hbm.1, bf16[32,64,128]{2,1,0:T(8,128)(2,1)} %bitcast.14), custom_call_target="tpu_custom_call" | custom-call | tf_op jit(solution)/shard_map/moments/pallas_call | solution.py:259
  2.1 8.8 %all-gather = f32[4,5,32,128]{3,2,1,0:T(8,128)S(1)} all-gather(f32[2,5,32,128]{3,2,1,0:T(8,128)} %moments.1), channel_id=2, replica_groups=mesh['z'=8,'xl'=2,'y'=8,'xh'=2,'core'=2] {'core'}, dimensions={0}, use_global_device_ids=true | all-gather | bytes 491520 | tf_op jit(solution)/shard_map/all_gather | solution.py:276
  10.8 0.0 copy-start
  10.8 0.7 %chip_sum.1 = bf16[8,5,16,128]{3,2,1,0:T(8,128)(2,1)} custom-call(s32[1]{0:T(128)} %bitcast.1.plane_ref, f32[2,2,5,32,128]{4,3,2,1,0:T(8,128)S(1)} %bitcast.18), custom_call_target="tpu_custom_call" | custom-call | tf_op jit(solution)/shard_map/chip_sum/pallas_call | solution.py:277
  11.5 3.4 %all-to-all-start = ((bf16[8,5,16,128]{3,2,1,0:T(8,128)(2,1)}), bf16[8,5,16,128]{3,2,1,0:T(8,128)(2,1)S(1)}, u32[]{:S(2)}, u32[]{:S(2)}) async-start(bf16[8,5,16,128]{3,2,1,0:T(8,128)(2,1)} %chip_sum.1), calls=%async_computation | async-start | bytes 327680 | tf_op jit(solution)/shard_map/all_to_all | solution.py:285
  14.9 0.0 copy-done
  14.9 0.3 split_planes.1
  15.2 1.9 %collective-permute-start = (bf16[32,32,128]{2,1,0:T(8,128)(2,1)S(1)}, bf16[32,32,128]{2,1,0:T(8,128)(2,1)S(1)}, u32[]{:S(2)}, u32[]{:S(2)}) collective-permute-start(bf16[32,32,128]{2,1,0:T(8,128)(2,1)S(1)} %get-tuple-element.14), channel_id=1, source_target_pairs={{0,32},{32,0},{64,96},{96,64},{128,160},{160,128},{192,224},{224,1... | collective-permute-start | bytes 786440 | tf_op jit(solution)/shard_map/ppermute | solution.py:313
  17.1 3.4 %collective-permute-start.2 = (bf16[32,32,128]{2,1,0:T(8,128)(2,1)S(1)}, bf16[32,32,128]{2,1,0:T(8,128)(2,1)S(1)}, u32[]{:S(2)}, u32[]{:S(2)}) collective-permute-start(bf16[32,32,128]{2,1,0:T(8,128)(2,1)S(1)} %get-tuple-element.15), channel_id=1, source_target_pairs={{0,32},{32,0},{64,96},{96,64},{128,160},{160,128},{192,224},{224,1... | collective-permute-start | bytes 786440 | tf_op jit(solution)/shard_map/ppermute | solution.py:314
  20.5 3.4 %all-to-all-done.parts_ref = bf16[8,5,16,128]{3,2,1,0:T(8,128)(2,1)S(1)} async-done(((bf16[8,5,16,128]{3,2,1,0:T(8,128)(2,1)}), bf16[8,5,16,128]{3,2,1,0:T(8,128)(2,1)S(1)}, u32[]{:S(2)}, u32[]{:S(2)}) %all-to-all-start) | async-done | bytes 163872 | tf_op jit(solution)/shard_map/all_to_all | solution.py:285
  24.0 0.8 %column_sum.1 = f32[8,5,16,128]{3,2,1,0:T(8,128)} custom-call(bf16[8,5,16,128]{3,2,1,0:T(8,128)(2,1)S(1)} %all-to-all-done.parts_ref), custom_call_target="tpu_custom_call" | custom-call | tf_op jit(solution)/shard_map/column_sum/pallas_call | solution.py:316
  24.7 10.7 %all-to-all-start.1 = ((f32[8,5,16,128]{3,2,1,0:T(8,128)}), f32[8,5,16,128]{3,2,1,0:T(8,128)S(1)}, u32[]{:S(2)}, u32[]{:S(2)}) async-start(f32[8,5,16,128]{3,2,1,0:T(8,128)} %column_sum.1), calls=%async_computation.1 | async-start | bytes 655360 | tf_op jit(solution)/shard_map/all_to_all | solution.py:324
  35.4 0.0 collective-permute-done.in_ref
  35.4 1.9 %collective-permute-start.1 = (bf16[32,32,128]{2,1,0:T(8,128)(2,1)S(1)}, bf16[32,32,128]{2,1,0:T(8,128)(2,1)S(1)}, u32[]{:S(2)}, u32[]{:S(2)}) collective-permute-start(bf16[32,32,128]{2,1,0:T(8,128)(2,1)S(1)} %hand_on.2), channel_id=1, source_target_pairs={{0,64},{32,480},{64,128},{96,32},{128,192},{160,96},{192,256},{224... | collective-permute-start | bytes 786440 | tf_op jit(solution)/shard_map/ppermute | solution.py:313
  37.3 0.0 collective-permute-done.2.in_ref
  37.4 4.2 %all-to-all-done.1 = f32[8,5,16,128]{3,2,1,0:T(8,128)S(1)} async-done(((f32[8,5,16,128]{3,2,1,0:T(8,128)}), f32[8,5,16,128]{3,2,1,0:T(8,128)S(1)}, u32[]{:S(2)}, u32[]{:S(2)}) %all-to-all-start.1) | async-done | bytes 327712 | tf_op jit(solution)/shard_map/all_to_all | solution.py:324
  41.6 0.0 copy-start.1
  41.6 2.4 %all-gather.1 = f32[16,5,16,128]{3,2,1,0:T(8,128)S(1)} all-gather(f32[8,5,16,128]{3,2,1,0:T(8,128)S(1)} %all-to-all-done.1), channel_id=3, replica_groups=mesh['z'=8,'xl'=2,'y'=8,'xh'=2,'core'=2] {'core'}, dimensions={0}, use_global_device_ids=true | all-gather | bytes 983040 | tf_op jit(solution)/shard_map/all_gather | solution.py:325
  44.0 0.0 copy-done.1
  44.0 2.2 %inner.1 = (f32[32,64,128]{2,1,0:T(8,128)S(1)}, f32[32,128]{1,0:T(8,128)S(1)}, f32[32,32,128]{2,1,0:T(8,128)S(1)}, f32[2,6,32,128]{3,2,1,0:T(8,128)S(1)}) custom-call(s32[1]{0:T(128)} %bitcast.side_ref, s32[3,32]{1,0:T(4,128)S(1)} %copy-done.1, f32[2,8,5,16,128]{4,3,2,1,0:T(8,128)S(1)} %bitcast.17, bf16[32,64,128]{2,1,0:T(8,128)(2,1)S(1)} %bitcast.16), custom_call_target="tpu_custom_call" | custom-call | flops 1 | bytes 1 | tf_op jit(solution)/shard_map/inner/pallas_call | solution.py:326
  46.1 0.1 collective-permute-done.1.across_ref
  46.2 1.1 %edge.1 = bf16[32,64,128]{2,1,0:T(8,128)(2,1)} custom-call(s32[1]{0:T(128)} %bitcast.side_ref, f32[32,128]{1,0:T(8,128)S(1)} %get-tuple-element.11.table_ref, f32[32,32,128]{2,1,0:T(8,128)S(1)} %get-tuple-element.12.equil_ref, f32[2,6,32,128]{3,2,1,0:T(8,128)S(1)} %get-tuple-element.13.edge_params_ref, ...), custom_call_target="tpu_custom_call" | custom-call | tf_op jit(solution)/shard_map/edge/pallas_call | solution.py:341
  (2 shorter events, 0.0 us)
Async XLA Ops:
  10.8 4.1 %copy-start = (bf16[32,2,4096]{2,1,0:T(2,128)(2,1)S(1)}, bf16[32,2,4096]{2,1,0:T(2,128)(2,1)}, u32[]{:S(2)}) copy-start(bf16[32,2,4096]{2,1,0:T(2,128)(2,1)} %param.3) | copy-start | bytes 1572868
  11.5 12.4 %all-to-all-start = ((bf16[8,5,16,128]{3,2,1,0:T(8,128)(2,1)}), bf16[8,5,16,128]{3,2,1,0:T(8,128)(2,1)S(1)}, u32[]{:S(2)}, u32[]{:S(2)}) async-start(bf16[8,5,16,128]{3,2,1,0:T(8,128)(2,1)} %chip_sum.1), calls=%async_computation | async-start | bytes 327680 | tf_op jit(solution)/shard_map/all_to_all | solution.py:285
  15.2 20.2 %collective-permute-start = (bf16[32,32,128]{2,1,0:T(8,128)(2,1)S(1)}, bf16[32,32,128]{2,1,0:T(8,128)(2,1)S(1)}, u32[]{:S(2)}, u32[]{:S(2)}) collective-permute-start(bf16[32,32,128]{2,1,0:T(8,128)(2,1)S(1)} %get-tuple-element.14), channel_id=1, source_target_pairs={{0,32},{32,0},{64,96},{96,64},{128,160},{160,128},{192,224},{224,1... | collective-permute-start | bytes 786440 | tf_op jit(solution)/shard_map/ppermute | solution.py:313
  17.1 20.2 %collective-permute-start.2 = (bf16[32,32,128]{2,1,0:T(8,128)(2,1)S(1)}, bf16[32,32,128]{2,1,0:T(8,128)(2,1)S(1)}, u32[]{:S(2)}, u32[]{:S(2)}) collective-permute-start(bf16[32,32,128]{2,1,0:T(8,128)(2,1)S(1)} %get-tuple-element.15), channel_id=1, source_target_pairs={{0,32},{32,0},{64,96},{96,64},{128,160},{160,128},{192,224},{224,1... | collective-permute-start | bytes 786440 | tf_op jit(solution)/shard_map/ppermute | solution.py:314
  24.7 16.9 %all-to-all-start.1 = ((f32[8,5,16,128]{3,2,1,0:T(8,128)}), f32[8,5,16,128]{3,2,1,0:T(8,128)S(1)}, u32[]{:S(2)}, u32[]{:S(2)}) async-start(f32[8,5,16,128]{3,2,1,0:T(8,128)} %column_sum.1), calls=%async_computation.1 | async-start | bytes 655360 | tf_op jit(solution)/shard_map/all_to_all | solution.py:324
  35.4 10.8 %collective-permute-start.1 = (bf16[32,32,128]{2,1,0:T(8,128)(2,1)S(1)}, bf16[32,32,128]{2,1,0:T(8,128)(2,1)S(1)}, u32[]{:S(2)}, u32[]{:S(2)}) collective-permute-start(bf16[32,32,128]{2,1,0:T(8,128)(2,1)S(1)} %hand_on.2), channel_id=1, source_target_pairs={{0,64},{32,480},{64,128},{96,32},{128,192},{160,96},{192,256},{224... | collective-permute-start | bytes 786440 | tf_op jit(solution)/shard_map/ppermute | solution.py:313
  41.6 2.4 %copy-start.1 = (s32[3,32]{1,0:T(4,128)S(1)}, s32[3,32]{1,0:T(4,128)}, u32[]{:S(2)}) copy-start(s32[3,32]{1,0:T(4,128)} %index_ref.1) | copy-start | bytes 1156

commit v6 on v5

--- a/solution.py
+++ b/solution.py
@@ -25,6 +25,7 @@
 VERT = ("y", "xh", "core")
 
 VMEM = pl.BlockSpec(memory_space=pltpu.VMEM)
+ANY = pl.BlockSpec(memory_space=pl.ANY)
 HBM = pl.BlockSpec(memory_space=pltpu.HBM)
 SMEM = pl.BlockSpec(memory_space=pltpu.SMEM)
 
@@ -108,18 +109,28 @@
             out_ref[y, comp] = total[first:first + HALF]
 
 
-def copy_kernel(in_ref, out_ref):
-    out_ref[...] = in_ref[...]
-
-
-def split_kernel(side_ref, dist_ref, far_ref, near_ref, rows_ref):
+def far_kernel(side_ref, dist_ref, far_ref, rows_ref):
     side = side_ref[0]
 
     def step(v, carry):
         slot = v & 3
         rows_ref[slot] = dist_ref[v].astype(jnp.float32)
         far_ref[v] = rows_ref[slot, pl.ds(side, ROWS, stride=2), :].astype(jnp.bfloat16)
-        near_ref[v] = rows_ref[slot, pl.ds(1 - side, ROWS, stride=2), :].astype(jnp.bfloat16)
+        return carry
+
+    lax.fori_loop(0, dist_ref.shape[0], step, 0, unroll=4)
+
+
+def merge_kernel(side_ref, index_ref, dist_ref, passed_ref, sent_ref, node_ref, rows_ref):
+    side = side_ref[0]
+    fill_nodes(node_ref)
+
+    def step(v, carry):
+        slot = v & 3
+        up = jnp.where(node_ref[index_ref[0, v]] > 0.0, 1, 0)
+        rows_ref[slot] = dist_ref[v].astype(jnp.float32)
+        own = rows_ref[slot, pl.ds(1 - side, ROWS, stride=2), :].astype(jnp.bfloat16)
+        sent_ref[v] = jnp.where(up == side, passed_ref[v], own)
         return carry
 
     lax.fori_loop(0, dist_ref.shape[0], step, 0, unroll=4)
@@ -146,10 +157,12 @@
 
 
 def inner_kernel(
-    side_ref, index_ref, sums_ref, dist_ref,
-    moved_ref, table_ref, equil_ref, edge_params_ref, node_ref, own_ref,
+    side_ref, index_any, sums_ref, dist_ref,
+    moved_ref, table_ref, equil_ref, edge_params_ref, index_ref, node_ref, own_ref, sem,
 ):
     side = side_ref[0]
+    indices = pltpu.make_async_copy(index_any, index_ref, sem.at[0])
+    indices.start()
     fill_nodes(node_ref)
     for plane, part in [(plane, part) for plane in range(4) for part in range(2)]:
         core, first = plane // 2, 4 * (plane % 2) + 2 * part
@@ -171,6 +184,7 @@
             else:
                 edge_params_ref[plane // 3, comp, pl.ds(HALF * part, HALF), :] = values[comp]
 
+    indices.wait()
     lane = lax.broadcasted_iota(jnp.int32, (8, LANES), 1)
     row = lax.broadcasted_iota(jnp.int32, (8, LANES), 0)
     column, upper, parity = lane & 63, lane >> 6, row & 1
@@ -213,7 +227,7 @@
 
 
 def edge_kernel(
-    side_ref, table_ref, equil_ref, edge_params_ref, across_ref, within_ref, moved_ref, out_hbm,
+    side_ref, table_ref, equil_ref, edge_params_ref, halo_ref, moved_ref, out_hbm,
     out_ref, edge_ref, sems,
 ):
     side = side_ref[0]
@@ -221,12 +235,12 @@
     keep_within = edge_params_ref[1 - side, 5]
     far_rows = (lax.broadcasted_iota(jnp.int32, BOTH, 0) & 1) == side
     copies = sems.shape[0]
-    count = across_ref.shape[0] // copies
+    count = halo_ref.shape[0] // copies
 
     def step(v, slot):
         size = table_ref[pl.ds(v, 1), :]
         far = size > 0.0
-        value = jnp.where(far, across_ref[v].astype(jnp.float32), within_ref[v].astype(jnp.float32))
+        value = halo_ref[v].astype(jnp.float32)
         mixed = value * jnp.where(far, keep_across, keep_within) + equil_ref[v]
         edge = mixed.astype(jnp.bfloat16).astype(jnp.float32) * jnp.abs(size)
         edge_ref[slot, pl.ds(0, ROWS, stride=2), :] = edge
@@ -286,32 +300,30 @@
 
     count = SIZES[0] * SIZES[1]
     swap = [(i, i ^ 1) for i in range(count)]
-    along = [(i, (i + 2 - 4 * (i % 2)) % count) for i in range(count)]
+    along = [(i, (i - 2 + 4 * (i % 2)) % count) for i in range(count)]
     half = jax.ShapeDtypeStruct((count_v,) + CELLS, bf16)
-    far, near = pl.pallas_call(
-        split_kernel,
-        out_shape=(half, half),
+    far = pl.pallas_call(
+        far_kernel,
+        out_shape=half,
         in_specs=[SMEM, VMEM],
-        out_specs=(VMEM, VMEM),
+        out_specs=VMEM,
         scratch_shapes=[pltpu.VMEM((4,) + BOTH, f32)],
         compiler_params=small(8),
         cost_estimate=pl.CostEstimate(flops=1 << 20, bytes_accessed=1 << 20, transcendentals=0),
-        name="split_planes",
+        name="far_planes",
     )(side, mixed)
-
-    def hand_on(planes, cost):
-        return pl.pallas_call(
-            copy_kernel,
-            out_shape=half,
-            in_specs=[VMEM],
-            out_specs=VMEM,
-            compiler_params=small(8),
-            cost_estimate=pl.CostEstimate(flops=cost, bytes_accessed=1 << 19, transcendentals=0),
-            name="hand_on",
-        )(planes)
-
-    across = lax.ppermute(hand_on(lax.ppermute(far, GX, swap), 1 << 31), GX, along)
-    within = hand_on(lax.ppermute(near, GX, swap), 1 << 32)
+    passed = lax.ppermute(far, GX, along)
+    sent = pl.pallas_call(
+        merge_kernel,
+        out_shape=half,
+        in_specs=[SMEM, SMEM, VMEM, VMEM],
+        out_specs=VMEM,
+        scratch_shapes=[pltpu.SMEM((NODES,), f32), pltpu.VMEM((4,) + BOTH, f32)],
+        compiler_params=small(8),
+        cost_estimate=pl.CostEstimate(flops=1 << 32, bytes_accessed=1 << 20, transcendentals=0),
+        name="upwind_planes",
+    )(side, vel_index, mixed, passed)
+    halo = lax.ppermute(sent, GX, swap)
 
     column = pl.pallas_call(
         column_kernel,
@@ -331,9 +343,14 @@
             jax.ShapeDtypeStruct((count_v,) + CELLS, f32),
             jax.ShapeDtypeStruct((2, 6) + CELLS, f32),
         ),
-        in_specs=[SMEM, SMEM, VMEM, VMEM],
+        in_specs=[SMEM, ANY, VMEM, VMEM],
         out_specs=(VMEM, VMEM, VMEM, VMEM),
-        scratch_shapes=[pltpu.SMEM((NODES,), f32), pltpu.VMEM((6,) + BOTH, f32)],
+        scratch_shapes=[
+            pltpu.SMEM(vel_index.shape, jnp.int32),
+            pltpu.SMEM((NODES,), f32),
+            pltpu.VMEM((6,) + BOTH, f32),
+            pltpu.SemaphoreType.DMA((1,)),
+        ],
         compiler_params=small(8),
         cost_estimate=pl.CostEstimate(flops=1, bytes_accessed=1, transcendentals=0),
         name="inner",
@@ -341,7 +358,7 @@
     out = pl.pallas_call(
         edge_kernel,
         out_shape=jax.ShapeDtypeStruct(mixed.shape, bf16),
-        in_specs=[SMEM, VMEM, VMEM, VMEM, VMEM, VMEM, VMEM],
+        in_specs=[SMEM, VMEM, VMEM, VMEM, VMEM, VMEM],
         out_specs=HBM,
         scratch_shapes=[
             pltpu.VMEM(mixed.shape, bf16),
@@ -350,7 +367,7 @@
         ],
         compiler_params=small(8),
         name="edge",
-    )(side, table, equil, edge_params, across, within, moved)
+    )(side, table, equil, edge_params, halo, moved)
     return out.reshape(count_v, ROWS, 2, LANES).transpose(0, 2, 1, 3).reshape(dist.shape)
 
 

time: 47.8 us -> 47.5 us (level)
  waiting for transfers between devices: 7.75 us -> 3.47 us
  starting transfers between devices: 21.2 us -> 24.8 us
  Pallas kernels: 7.09 us -> 7.76 us
    ppermute x3 -> x2, starting transfers between devices: 7.2 us -> 10.6 us  [the longest x1 8.72 us: shards(): passed = lax.ppermute(far, GX, along)]
    all_to_all x1, waiting for transfers between devices: 3.45 us -> 0.05 us  [shards(): parts = lax.all_to_all(chip, 'y', 0, 0)]
    all_to_all x1, waiting for transfers between devices: 4.21 us -> 3.41 us  [shards(): gathered = lax.all_to_all(column, NAMES, 0, 0, axis_index_groups=GROUPS)]
    pallas_call x3 -> x2, Pallas kernels: 0.34 us -> 1.12 us  [the longest x1 0.85 us: shards(): pl.pallas_call(merge_kernel, out_shape=half, in_specs=[SMEM, SMEM, VMEM,...]
  transfers between devices with their start and end apart: 5 -> 4, of which waited for: 3 -> 2; matrix products, arithmetic and copies ran while one was open for 0% -> 0% of each run, Pallas kernels for 7% -> 8%
where the time goes in v6:
time: 47.5 us; the launch traced here: 47.1 us
  starting transfers between devices  24.8 us (52%)
  blocking collectives  11 us (23%)
  Pallas kernels  7.76 us (16%)
  waiting for transfers between devices  3.47 us (7%)
    all_to_all x1, starting transfers between devices, shards(): gathered = lax.all_to_all(column, NAMES, 0, 0, axis_index_groups=GROUPS)  10.8 us
    all_gather x1, blocking collectives, shards(): both = lax.all_gather(partial_sums, 'core')  8.76 us
    ppermute x1, starting transfers between devices, shards(): passed = lax.ppermute(far, GX, along)  8.72 us
    all_to_all x1, waiting for transfers between devices, shards(): gathered = lax.all_to_all(column, NAMES, 0, 0, axis_index_groups=GROUPS)  3.41 us
    all_to_all x1, starting transfers between devices, shards(): parts = lax.all_to_all(chip, 'y', 0, 0)  3.38 us
    all_gather x1, blocking collectives, shards(): sums = lax.all_gather(gathered, 'core')  2.26 us
    pallas_call x1, Pallas kernels, shards(): pl.pallas_call(moments_kernel, out_shape=jax.ShapeDtypeStruct((2, 5) + CE...  2.07 us
    pallas_call x1, Pallas kernels, shards(): pl.pallas_call(inner_kernel, out_shape=(jax.ShapeDtypeStruct(mixed.shape,...  2.06 us
  transfers between devices with their start and end apart: 4, of which 2 were waited for; matrix products, arithmetic and copies ran while one was open for 0% of the time, Pallas kernels for 8%

profile of v6, /device:TPU:1, one launch (start us, length us, event | category | flops | bytes accessed | tf_op | source)
XLA Modules:
  0.0 47.1 jit_solution(11536848502304623158)
XLA Ops:
  0.0 2.1 %moments.1 = f32[2,5,32,128]{3,2,1,0:T(8,128)} custom-call(s32[3,32]{1,0:T(4,128)} %index_ref.1, s32[32]{0:T(128)} %weight_hbm.1, bf16[32,64,128]{2,1,0:T(8,128)(2,1)} %bitcast.14), custom_call_target="tpu_custom_call" | custom-call | tf_op jit(solution)/shard_map/moments/pallas_call | solution.py:273
  2.1 8.8 %all-gather = f32[4,5,32,128]{3,2,1,0:T(8,128)S(1)} all-gather(f32[2,5,32,128]{3,2,1,0:T(8,128)} %moments.1), channel_id=2, replica_groups=mesh['z'=8,'xl'=2,'y'=8,'xh'=2,'core'=2] {'core'}, dimensions={0}, use_global_device_ids=true | all-gather | bytes 491520 | tf_op jit(solution)/shard_map/all_gather | solution.py:290
  10.8 0.0 copy-start
  10.8 0.7 %chip_sum.1 = bf16[8,5,16,128]{3,2,1,0:T(8,128)(2,1)} custom-call(s32[1]{0:T(128)} %bitcast.1.plane_ref, f32[2,2,5,32,128]{4,3,2,1,0:T(8,128)S(1)} %bitcast.19), custom_call_target="tpu_custom_call" | custom-call | tf_op jit(solution)/shard_map/chip_sum/pallas_call | solution.py:291
  11.5 3.4 %all-to-all-start = ((bf16[8,5,16,128]{3,2,1,0:T(8,128)(2,1)}), bf16[8,5,16,128]{3,2,1,0:T(8,128)(2,1)S(1)}, u32[]{:S(2)}, u32[]{:S(2)}) async-start(bf16[8,5,16,128]{3,2,1,0:T(8,128)(2,1)} %chip_sum.1), calls=%async_computation | async-start | bytes 327680 | tf_op jit(solution)/shard_map/all_to_all | solution.py:299
  14.9 0.0 copy-done
  14.9 0.3 far_planes.1
  15.2 8.7 %collective-permute-start = (bf16[32,32,128]{2,1,0:T(8,128)(2,1)S(1)}, bf16[32,32,128]{2,1,0:T(8,128)(2,1)S(1)}, u32[]{:S(2)}, u32[]{:S(2)}) collective-permute-start(bf16[32,32,128]{2,1,0:T(8,128)(2,1)S(1)} %far_planes.1), channel_id=1, source_target_pairs={{0,448},{32,96},{64,0},{96,160},{128,64},{160,224},{192,128},{224,... | collective-permute-start | bytes 786440 | tf_op jit(solution)/shard_map/ppermute | solution.py:315
  23.9 0.1 all-to-all-done.parts_ref
  24.0 0.8 %column_sum.1 = f32[8,5,16,128]{3,2,1,0:T(8,128)} custom-call(bf16[8,5,16,128]{3,2,1,0:T(8,128)(2,1)S(1)} %all-to-all-done.parts_ref), custom_call_target="tpu_custom_call" | custom-call | tf_op jit(solution)/shard_map/column_sum/pallas_call | solution.py:328
  24.7 0.0 copy-start.1
  24.7 10.8 %all-to-all-start.1 = ((f32[8,5,16,128]{3,2,1,0:T(8,128)}), f32[8,5,16,128]{3,2,1,0:T(8,128)S(1)}, u32[]{:S(2)}, u32[]{:S(2)}) async-start(f32[8,5,16,128]{3,2,1,0:T(8,128)} %column_sum.1), calls=%async_computation.1 | async-start | bytes 655360 | tf_op jit(solution)/shard_map/all_to_all | solution.py:336
  35.5 0.0 collective-permute-done.passed_ref
  35.5 0.0 copy-done.1
  35.5 0.9 %upwind_planes.1 = bf16[32,32,128]{2,1,0:T(8,128)(2,1)S(1)} custom-call(s32[1]{0:T(128)} %bitcast.side_ref, s32[3,32]{1,0:T(4,128)S(1)} %copy-done.1, bf16[32,64,128]{2,1,0:T(8,128)(2,1)S(1)} %bitcast.16, bf16[32,32,128]{2,1,0:T(8,128)(2,1)S(1)} %collective-permute-done.passed_ref), custom_call_target="tpu_custom_call" | custom-call | flops 4294967296 | bytes 1048576 | tf_op jit(solution)/shard_map/upwind_planes/pallas_call | solution.py:316
  36.4 1.9 %collective-permute-start.1 = (bf16[32,32,128]{2,1,0:T(8,128)(2,1)S(1)}, bf16[32,32,128]{2,1,0:T(8,128)(2,1)S(1)}, u32[]{:S(2)}, u32[]{:S(2)}) collective-permute-start(bf16[32,32,128]{2,1,0:T(8,128)(2,1)S(1)} %upwind_planes.1), channel_id=1, source_target_pairs={{0,32},{32,0},{64,96},{96,64},{128,160},{160,128},{192,224},{224,1... | collective-permute-start | bytes 786440 | tf_op jit(solution)/shard_map/ppermute | solution.py:326
  38.3 3.4 %all-to-all-done.1 = f32[8,5,16,128]{3,2,1,0:T(8,128)S(1)} async-done(((f32[8,5,16,128]{3,2,1,0:T(8,128)}), f32[8,5,16,128]{3,2,1,0:T(8,128)S(1)}, u32[]{:S(2)}, u32[]{:S(2)}) %all-to-all-start.1) | async-done | bytes 327712 | tf_op jit(solution)/shard_map/all_to_all | solution.py:336
  41.7 2.3 %all-gather.1 = f32[16,5,16,128]{3,2,1,0:T(8,128)S(1)} all-gather(f32[8,5,16,128]{3,2,1,0:T(8,128)S(1)} %all-to-all-done.1), channel_id=3, replica_groups=mesh['z'=8,'xl'=2,'y'=8,'xh'=2,'core'=2] {'core'}, dimensions={0}, use_global_device_ids=true | all-gather | bytes 983040 | tf_op jit(solution)/shard_map/all_gather | solution.py:337
  44.0 2.1 %inner.1 = (f32[32,64,128]{2,1,0:T(8,128)S(1)}, f32[32,128]{1,0:T(8,128)S(1)}, f32[32,32,128]{2,1,0:T(8,128)S(1)}, f32[2,6,32,128]{3,2,1,0:T(8,128)S(1)}) custom-call(s32[1]{0:T(128)} %bitcast.side_ref, s32[3,32]{1,0:T(4,128)S(1)} %copy-done.1, f32[2,8,5,16,128]{4,3,2,1,0:T(8,128)S(1)} %bitcast.18, bf16[32,64,128]{2,1,0:T(8,128)(2,1)S(1)} %bitcast.17), custom_call_target="tpu_custom_call" | custom-call | flops 1 | bytes 1 | tf_op jit(solution)/shard_map/inner/pallas_call | solution.py:338
  46.0 0.0 collective-permute-done.1.halo_ref
  46.1 1.1 %edge.1 = bf16[32,64,128]{2,1,0:T(8,128)(2,1)} custom-call(s32[1]{0:T(128)} %bitcast.side_ref, f32[32,128]{1,0:T(8,128)S(1)} %get-tuple-element.9.table_ref, f32[32,32,128]{2,1,0:T(8,128)S(1)} %get-tuple-element.10.equil_ref, f32[2,6,32,128]{3,2,1,0:T(8,128)S(1)} %get-tuple-element.11.edge_params_ref, ...), custom_call_target="tpu_custom_call" | custom-call | tf_op jit(solution)/shard_map/edge/pallas_call | solution.py:358
Async XLA Ops:
  10.8 4.1 %copy-start = (bf16[32,2,4096]{2,1,0:T(2,128)(2,1)S(1)}, bf16[32,2,4096]{2,1,0:T(2,128)(2,1)}, u32[]{:S(2)}) copy-start(bf16[32,2,4096]{2,1,0:T(2,128)(2,1)} %param.3) | copy-start | bytes 1572868
  11.5 12.4 %all-to-all-start = ((bf16[8,5,16,128]{3,2,1,0:T(8,128)(2,1)}), bf16[8,5,16,128]{3,2,1,0:T(8,128)(2,1)S(1)}, u32[]{:S(2)}, u32[]{:S(2)}) async-start(bf16[8,5,16,128]{3,2,1,0:T(8,128)(2,1)} %chip_sum.1), calls=%async_computation | async-start | bytes 327680 | tf_op jit(solution)/shard_map/all_to_all | solution.py:299
  15.2 20.3 %collective-permute-start = (bf16[32,32,128]{2,1,0:T(8,128)(2,1)S(1)}, bf16[32,32,128]{2,1,0:T(8,128)(2,1)S(1)}, u32[]{:S(2)}, u32[]{:S(2)}) collective-permute-start(bf16[32,32,128]{2,1,0:T(8,128)(2,1)S(1)} %far_planes.1), channel_id=1, source_target_pairs={{0,448},{32,96},{64,0},{96,160},{128,64},{160,224},{192,128},{224,... | collective-permute-start | bytes 786440 | tf_op jit(solution)/shard_map/ppermute | solution.py:315
  24.7 10.8 %copy-start.1 = (s32[3,32]{1,0:T(4,128)S(1)}, s32[3,32]{1,0:T(4,128)}, u32[]{:S(2)}) copy-start(s32[3,32]{1,0:T(4,128)} %index_ref.1) | copy-start | bytes 1156
  24.7 17.0 %all-to-all-start.1 = ((f32[8,5,16,128]{3,2,1,0:T(8,128)}), f32[8,5,16,128]{3,2,1,0:T(8,128)S(1)}, u32[]{:S(2)}, u32[]{:S(2)}) async-start(f32[8,5,16,128]{3,2,1,0:T(8,128)} %column_sum.1), calls=%async_computation.1 | async-start | bytes 655360 | tf_op jit(solution)/shard_map/all_to_all | solution.py:336
  36.4 9.7 %collective-permute-start.1 = (bf16[32,32,128]{2,1,0:T(8,128)(2,1)S(1)}, bf16[32,32,128]{2,1,0:T(8,128)(2,1)S(1)}, u32[]{:S(2)}, u32[]{:S(2)}) collective-permute-start(bf16[32,32,128]{2,1,0:T(8,128)(2,1)S(1)} %upwind_planes.1), channel_id=1, source_target_pairs={{0,32},{32,0},{64,96},{96,64},{128,160},{160,128},{192,224},{224,1... | collective-permute-start | bytes 786440 | tf_op jit(solution)/shard_map/ppermute | solution.py:326

commit v7 on v6

--- a/solution.py
+++ b/solution.py
@@ -45,6 +45,7 @@
     for pair in PAIRS
     for y in range(0, SIZES[2], 2)
 ]
+MOMENTS_VMEM = 56254464
 NODE_SPEEDS = [float(speed_max * np.cos(np.pi * j / (NODES - 1))) for j in range(NODES)]
 
 
@@ -284,7 +285,7 @@
             pltpu.SemaphoreType.DMA((2,)),
             pltpu.SemaphoreType.DMA((4,)),
         ],
-        compiler_params=small(56),
+        compiler_params=pltpu.CompilerParams(vmem_limit_bytes=MOMENTS_VMEM),
         name="moments",
     )(vel_index, weight_int, mixed)
     both = lax.all_gather(partial_sums, "core")

time: 47.5 us -> 47.2 us (level)
  local copies, waits for them, and re-layouts: 0.01 us -> 0.69 us
  Pallas kernels: 7.76 us -> 7.1 us
    unnamed x4 -> x6, local copies, waits for them, and re-layouts: 0.01 us -> 0.69 us
    pallas_call x1, Pallas kernels: 2.07 us -> 1.4 us  [shards(): pl.pallas_call(moments_kernel, out_shape=jax.ShapeDtypeStruct((2, 5) + CE...]
where the time goes in v7:
time: 47.2 us; the launch traced here: 46.8 us
  starting transfers between devices  24.7 us (52%)
  blocking collectives  10.8 us (23%)
  Pallas kernels  7.1 us (15%)
  waiting for transfers between devices  3.47 us (7%)
  local copies, waits for them, and re-layouts  0.69 us (1%)
    all_to_all x1, starting transfers between devices, shards(): gathered = lax.all_to_all(column, NAMES, 0, 0, axis_index_groups=GROUPS)  10.7 us
    ppermute x1, starting transfers between devices, shards(): passed = lax.ppermute(far, GX, along)  8.72 us
    all_gather x1, blocking collectives, shards(): both = lax.all_gather(partial_sums, 'core')  8.55 us
    all_to_all x1, waiting for transfers between devices, shards(): gathered = lax.all_to_all(column, NAMES, 0, 0, axis_index_groups=GROUPS)  3.42 us
    all_to_all x1, starting transfers between devices, shards(): parts = lax.all_to_all(chip, 'y', 0, 0)  3.38 us
    all_gather x1, blocking collectives, shards(): sums = lax.all_gather(gathered, 'core')  2.26 us
    pallas_call x1, Pallas kernels, shards(): pl.pallas_call(inner_kernel, out_shape=(jax.ShapeDtypeStruct(mixed.shape,...  2.06 us
    ppermute x1, starting transfers between devices, shards(): halo = lax.ppermute(sent, GX, swap)  1.92 us
  transfers between devices with their start and end apart: 4, of which 2 were waited for; matrix products, arithmetic and copies ran while one was open for 0% of the time, Pallas kernels for 8%

profile of v7, /device:TPU:1, one launch (start us, length us, event | category | flops | bytes accessed | tf_op | source)
XLA Modules:
  0.0 46.8 jit_solution(15932974240564973679)
XLA Ops:
  0.0 0.0 copy-start.1
  0.0 0.0 copy-start.2
  0.0 0.7 %copy-done.1 = s32[3,32]{1,0:T(4,128)S(1)} copy-done((s32[3,32]{1,0:T(4,128)S(1)}, s32[3,32]{1,0:T(4,128)}, u32[]{:S(2)}) %copy-start.1) | copy-done | bytes 408
  0.7 0.0 copy-done.2
  0.7 1.4 %moments.1 = f32[2,5,32,128]{3,2,1,0:T(8,128)S(1)} custom-call(s32[3,32]{1,0:T(4,128)S(1)} %copy-done.1, s32[32]{0:T(128)S(1)} %copy-done.2, bf16[32,64,128]{2,1,0:T(8,128)(2,1)} %bitcast.14), custom_call_target="tpu_custom_call" | custom-call | tf_op jit(solution)/shard_map/moments/pallas_call | solution.py:274
  2.1 8.6 %all-gather = f32[4,5,32,128]{3,2,1,0:T(8,128)S(1)} all-gather(f32[2,5,32,128]{3,2,1,0:T(8,128)S(1)} %moments.1), channel_id=2, replica_groups=mesh['z'=8,'xl'=2,'y'=8,'xh'=2,'core'=2] {'core'}, dimensions={0}, use_global_device_ids=true | all-gather | bytes 491520 | tf_op jit(solution)/shard_map/all_gather | solution.py:291
  10.6 0.0 copy-start
  10.7 0.7 %chip_sum.1 = bf16[8,5,16,128]{3,2,1,0:T(8,128)(2,1)} custom-call(s32[1]{0:T(128)} %bitcast.1.plane_ref, f32[2,2,5,32,128]{4,3,2,1,0:T(8,128)S(1)} %bitcast.19), custom_call_target="tpu_custom_call" | custom-call | tf_op jit(solution)/shard_map/chip_sum/pallas_call | solution.py:292
  11.3 3.4 %all-to-all-start = ((bf16[8,5,16,128]{3,2,1,0:T(8,128)(2,1)}), bf16[8,5,16,128]{3,2,1,0:T(8,128)(2,1)S(1)}, u32[]{:S(2)}, u32[]{:S(2)}) async-start(bf16[8,5,16,128]{3,2,1,0:T(8,128)(2,1)} %chip_sum.1), calls=%async_computation | async-start | bytes 327680 | tf_op jit(solution)/shard_map/all_to_all | solution.py:300
  14.7 0.0 copy-done
  14.7 0.3 far_planes.1
  15.0 8.7 %collective-permute-start = (bf16[32,32,128]{2,1,0:T(8,128)(2,1)S(1)}, bf16[32,32,128]{2,1,0:T(8,128)(2,1)S(1)}, u32[]{:S(2)}, u32[]{:S(2)}) collective-permute-start(bf16[32,32,128]{2,1,0:T(8,128)(2,1)S(1)} %far_planes.1), channel_id=1, source_target_pairs={{0,448},{32,96},{64,0},{96,160},{128,64},{160,224},{192,128},{224,... | collective-permute-start | bytes 786440 | tf_op jit(solution)/shard_map/ppermute | solution.py:316
  23.7 0.1 all-to-all-done.parts_ref
  23.8 0.8 %column_sum.1 = f32[8,5,16,128]{3,2,1,0:T(8,128)} custom-call(bf16[8,5,16,128]{3,2,1,0:T(8,128)(2,1)S(1)} %all-to-all-done.parts_ref), custom_call_target="tpu_custom_call" | custom-call | tf_op jit(solution)/shard_map/column_sum/pallas_call | solution.py:329
  24.5 10.7 %all-to-all-start.1 = ((f32[8,5,16,128]{3,2,1,0:T(8,128)}), f32[8,5,16,128]{3,2,1,0:T(8,128)S(1)}, u32[]{:S(2)}, u32[]{:S(2)}) async-start(f32[8,5,16,128]{3,2,1,0:T(8,128)} %column_sum.1), calls=%async_computation.1 | async-start | bytes 655360 | tf_op jit(solution)/shard_map/all_to_all | solution.py:337
  35.2 0.0 collective-permute-done.passed_ref
  35.2 0.9 %upwind_planes.1 = bf16[32,32,128]{2,1,0:T(8,128)(2,1)S(1)} custom-call(s32[1]{0:T(128)} %bitcast.side_ref, s32[3,32]{1,0:T(4,128)S(1)} %copy-done.1, bf16[32,64,128]{2,1,0:T(8,128)(2,1)S(1)} %bitcast.16, bf16[32,32,128]{2,1,0:T(8,128)(2,1)S(1)} %collective-permute-done.passed_ref), custom_call_target="tpu_custom_call" | custom-call | flops 4294967296 | bytes 1048576 | tf_op jit(solution)/shard_map/upwind_planes/pallas_call | solution.py:317
  36.0 1.9 %collective-permute-start.1 = (bf16[32,32,128]{2,1,0:T(8,128)(2,1)S(1)}, bf16[32,32,128]{2,1,0:T(8,128)(2,1)S(1)}, u32[]{:S(2)}, u32[]{:S(2)}) collective-permute-start(bf16[32,32,128]{2,1,0:T(8,128)(2,1)S(1)} %upwind_planes.1), channel_id=1, source_target_pairs={{0,32},{32,0},{64,96},{96,64},{128,160},{160,128},{192,224},{224,1... | collective-permute-start | bytes 786440 | tf_op jit(solution)/shard_map/ppermute | solution.py:327
  38.0 3.4 %all-to-all-done.1 = f32[8,5,16,128]{3,2,1,0:T(8,128)S(1)} async-done(((f32[8,5,16,128]{3,2,1,0:T(8,128)}), f32[8,5,16,128]{3,2,1,0:T(8,128)S(1)}, u32[]{:S(2)}, u32[]{:S(2)}) %all-to-all-start.1) | async-done | bytes 327712 | tf_op jit(solution)/shard_map/all_to_all | solution.py:337
  41.4 2.3 %all-gather.1 = f32[16,5,16,128]{3,2,1,0:T(8,128)S(1)} all-gather(f32[8,5,16,128]{3,2,1,0:T(8,128)S(1)} %all-to-all-done.1), channel_id=3, replica_groups=mesh['z'=8,'xl'=2,'y'=8,'xh'=2,'core'=2] {'core'}, dimensions={0}, use_global_device_ids=true | all-gather | bytes 983040 | tf_op jit(solution)/shard_map/all_gather | solution.py:338
  43.7 2.1 %inner.1 = (f32[32,64,128]{2,1,0:T(8,128)S(1)}, f32[32,128]{1,0:T(8,128)S(1)}, f32[32,32,128]{2,1,0:T(8,128)S(1)}, f32[2,6,32,128]{3,2,1,0:T(8,128)S(1)}) custom-call(s32[1]{0:T(128)} %bitcast.side_ref, s32[3,32]{1,0:T(4,128)S(1)} %copy-done.1, f32[2,8,5,16,128]{4,3,2,1,0:T(8,128)S(1)} %bitcast.18, bf16[32,64,128]{2,1,0:T(8,128)(2,1)S(1)} %bitcast.17), custom_call_target="tpu_custom_call" | custom-call | flops 1 | bytes 1 | tf_op jit(solution)/shard_map/inner/pallas_call | solution.py:339
  45.7 0.0 collective-permute-done.1.halo_ref
  45.7 1.1 %edge.1 = bf16[32,64,128]{2,1,0:T(8,128)(2,1)} custom-call(s32[1]{0:T(128)} %bitcast.side_ref, f32[32,128]{1,0:T(8,128)S(1)} %get-tuple-element.9.table_ref, f32[32,32,128]{2,1,0:T(8,128)S(1)} %get-tuple-element.10.equil_ref, f32[2,6,32,128]{3,2,1,0:T(8,128)S(1)} %get-tuple-element.11.edge_params_ref, ...), custom_call_target="tpu_custom_call" | custom-call | tf_op jit(solution)/shard_map/edge/pallas_call | solution.py:359
Async XLA Ops:
  0.0 0.7 %copy-start.1 = (s32[3,32]{1,0:T(4,128)S(1)}, s32[3,32]{1,0:T(4,128)}, u32[]{:S(2)}) copy-start(s32[3,32]{1,0:T(4,128)} %index_ref.1) | copy-start | bytes 1156
  0.0 0.7 %copy-start.2 = (s32[32]{0:T(128)S(1)}, s32[32]{0:T(128)}, u32[]{:S(2)}) copy-start(s32[32]{0:T(128)} %weight_hbm.1) | copy-start | bytes 388
  10.6 4.1 %copy-start = (bf16[32,2,4096]{2,1,0:T(2,128)(2,1)S(1)}, bf16[32,2,4096]{2,1,0:T(2,128)(2,1)}, u32[]{:S(2)}) copy-start(bf16[32,2,4096]{2,1,0:T(2,128)(2,1)} %param.3) | copy-start | bytes 1572868
  11.3 12.4 %all-to-all-start = ((bf16[8,5,16,128]{3,2,1,0:T(8,128)(2,1)}), bf16[8,5,16,128]{3,2,1,0:T(8,128)(2,1)S(1)}, u32[]{:S(2)}, u32[]{:S(2)}) async-start(bf16[8,5,16,128]{3,2,1,0:T(8,128)(2,1)} %chip_sum.1), calls=%async_computation | async-start | bytes 327680 | tf_op jit(solution)/shard_map/all_to_all | solution.py:300
  15.0 20.2 %collective-permute-start = (bf16[32,32,128]{2,1,0:T(8,128)(2,1)S(1)}, bf16[32,32,128]{2,1,0:T(8,128)(2,1)S(1)}, u32[]{:S(2)}, u32[]{:S(2)}) collective-permute-start(bf16[32,32,128]{2,1,0:T(8,128)(2,1)S(1)} %far_planes.1), channel_id=1, source_target_pairs={{0,448},{32,96},{64,0},{96,160},{128,64},{160,224},{192,128},{224,... | collective-permute-start | bytes 786440 | tf_op jit(solution)/shard_map/ppermute | solution.py:316
  24.5 16.9 %all-to-all-start.1 = ((f32[8,5,16,128]{3,2,1,0:T(8,128)}), f32[8,5,16,128]{3,2,1,0:T(8,128)S(1)}, u32[]{:S(2)}, u32[]{:S(2)}) async-start(f32[8,5,16,128]{3,2,1,0:T(8,128)} %column_sum.1), calls=%async_computation.1 | async-start | bytes 655360 | tf_op jit(solution)/shard_map/all_to_all | solution.py:337
  36.0 9.7 %collective-permute-start.1 = (bf16[32,32,128]{2,1,0:T(8,128)(2,1)S(1)}, bf16[32,32,128]{2,1,0:T(8,128)(2,1)S(1)}, u32[]{:S(2)}, u32[]{:S(2)}) collective-permute-start(bf16[32,32,128]{2,1,0:T(8,128)(2,1)S(1)} %upwind_planes.1), channel_id=1, source_target_pairs={{0,32},{32,0},{64,96},{96,64},{128,160},{160,128},{192,224},{224,1... | collective-permute-start | bytes 786440 | tf_op jit(solution)/shard_map/ppermute | solution.py:327
